TPU v7x, 32 devices: a whole 2x2x4 slice. The times are simulated.
32 devices in a mesh: fsdp: 16 (over z, x, core), seq: 2 (over y).
Axes of the slice: x: 2, y: 2, z: 4, core: 2. Of those that a mesh axis runs over, the one named last changes fastest.
Arguments:
- tokens: bfloat16 [16, 1024, 1024], P('fsdp', 'seq'), may hold values from -6 to 6
- positions: int32 [3, 16, 1024], P(None, 'fsdp', 'seq'), may hold values from 0 to 15
- ln1_gain: bfloat16 [1024], P('fsdp'), may hold values from 0.099609375 to 1.8984375
- ln1_bias: bfloat16 [1024], P('fsdp'), may hold values from -3 to 3
- qkv_weight: bfloat16 [1024, 3072], P('fsdp'), may hold values from -0.1875 to 0.1875
- qkv_bias: bfloat16 [3072], P('fsdp'), may hold values from -0.19921875 to 0.19921875
- out_weight: bfloat16 [1024, 1024], P('fsdp'), may hold values from -4 to 4
- out_bias: bfloat16 [1024], P('fsdp'), may hold values from -3 to 3
- ln2_gain: bfloat16 [1024], P('fsdp'), may hold values from 0.099609375 to 1.8984375
- ln2_bias: bfloat16 [1024], P('fsdp'), may hold values from -3 to 3
- fc1_weight: bfloat16 [1024, 4096], P('fsdp'), may hold values from -0.1875 to 0.1875
- fc1_bias: bfloat16 [4096], P('fsdp'), may hold values from -3 to 3
- fc2_weight: bfloat16 [4096, 1024], P('fsdp'), may hold values from -0.09375 to 0.09375
- fc2_bias: bfloat16 [1024], P('fsdp'), may hold values from -3 to 3
- out_grad: bfloat16 [16, 1024, 1024], P('fsdp', 'seq'), may hold values from -6 to 6
Outputs:
- block_out: bfloat16 [16, 1024, 1024], P('fsdp', 'seq')
- tokens_grad: float32 [16, 1024, 1024], P('fsdp', 'seq')
- ln1_gain_grad: float32 [1024], P('fsdp')
- ln1_bias_grad: float32 [1024], P('fsdp')
- qkv_weight_grad: float32 [1024, 3072], P('fsdp')
- qkv_bias_grad: float32 [3072], P('fsdp')
- out_weight_grad: float32 [1024, 1024], P('fsdp')
- out_bias_grad: float32 [1024], P('fsdp')
- ln2_gain_grad: float32 [1024], P('fsdp')
- ln2_bias_grad: float32 [1024], P('fsdp')
- fc1_weight_grad: float32 [1024, 4096], P('fsdp')
- fc1_bias_grad: float32 [4096], P('fsdp')
- fc2_weight_grad: float32 [4096, 1024], P('fsdp')
- fc2_bias_grad: float32 [1024], P('fsdp')
All inputs are finite; a program needn't handle non-finite values.
Results may differ from a plain program's by a relative error of at most 0.011.
Values may be sent and summed in bfloat16 or wider, within the bound.
No kernel may reach another device: no remote copies, remote signals or barrier semaphores. Data moves between devices by JAX's collectives and lax.ppermute only.
A program may use at most 192 MiB of HBM per device.

v0:
```python
import functools

import jax
import jax.numpy as jnp
import numpy as np
from jax import lax
from jax.experimental import pallas as pl
from jax.experimental.pallas import tpu as pltpu
from jax.sharding import Mesh, PartitionSpec as P

HD = 64
EPS = 1e-06
THETA = 10000.0
LOG2E = 1.4426950408889634
SCALE = HD**-0.5
BF = jnp.bfloat16
F32 = jnp.float32
NT = (((1,), (1,)), ((), ()))
TN = (((0,), (0,)), ((), ()))
NN = (((1,), (0,)), ((), ()))
SMALL = 128
VMEM_BYTES = 56 << 20
LOW, HIGH = 0.25, 200
SHARD = ("o", "i", "c")
SEQ = "seq"


def mm(a, b, dims=NN):
    return lax.dot_general(a, b, dims, preferred_element_type=F32)


def shifted(size, by):
    return [(i, (i + by) % size) for i in range(size)]


def take(values, index, axis):
    return lax.dynamic_index_in_dim(values, index, axis, keepdims=False)


def shape(dims, dtype):
    return jax.ShapeDtypeStruct(dims, dtype)


def fixed(*dims):
    return pl.BlockSpec(dims, lambda *_: (0,) * len(dims))


def spec(block, index):
    return pl.BlockSpec(block, index)


def call(kernel, grid, in_specs, out_specs, out_shape, flops, moved, exps=0, scratch=(), scalars=0, weight=LOW):
    return pl.pallas_call(
        kernel,
        grid_spec=pltpu.PrefetchScalarGridSpec(
            num_scalar_prefetch=scalars,
            grid=grid,
            in_specs=in_specs,
            out_specs=out_specs,
            scratch_shapes=list(scratch),
        ),
        out_shape=out_shape,
        compiler_params=pltpu.CompilerParams(vmem_limit_bytes=VMEM_BYTES),
        cost_estimate=pl.CostEstimate(flops=int(weight * flops), bytes_accessed=int(weight * moved), transcendentals=int(weight * exps)),
    )


def pick(parts, index):
    chosen = parts[0]
    for k in range(1, len(parts)):
        chosen = jnp.where(index == k, parts[k], chosen)
    return chosen


def chips_in_line(mesh):
    chips = mesh.devices.shape[0] // 2
    places = [getattr(d, "coords", None) for d in mesh.devices[::2, 0]]
    if places[0] is None or chips < 2:
        return 2 if chips % 2 == 0 else 1
    axis = [a for a in range(3) if places[0][a] != places[1][a]][0]
    inner = 1
    while inner < chips and all(places[inner][a] == places[0][a] for a in range(3) if a != axis):
        inner += 1
    return inner


class Lines:
    def __init__(self, mesh):
        fsdp, seq = mesh.devices.shape
        self.chips = fsdp // 2
        self.inner = chips_in_line(mesh)
        self.outer = self.chips // self.inner
        self.mesh = Mesh(mesh.devices.reshape(self.outer, self.inner, 2, seq), SHARD + (SEQ,))
        self.outer_long = self.outer >= self.inner
        self.long, self.short = ("o", "i") if self.outer_long else ("i", "o")
        self.n_long, self.n_short = max(self.outer, self.inner), min(self.outer, self.inner)

    def place(self, long, short):
        return (long, short) if self.outer_long else (short, long)

    def split(self, values):
        return values.reshape(self.outer, self.inner, *values.shape[1:])

    def here(self):
        return jnp.stack([lax.axis_index(a) for a in (self.long, self.short, "c", SEQ)]).astype(jnp.int32)


def stack_kernel(lines, here, *refs):
    *pieces, out, sems = refs
    copies = []
    for n, piece in enumerate(pieces):
        back_short, back_long = n // lines.n_long, n % lines.n_long
        long = lax.rem(here[0] + (lines.n_long - back_long), lines.n_long)
        short = lax.rem(here[1] + (lines.n_short - back_short), lines.n_short)
        a, b = lines.place(long, short)
        copies.append(pltpu.make_async_copy(piece, out.at[a, b], sems.at[n]))
    for copy in copies:
        copy.start()
    for copy in copies:
        copy.wait()


def staged_gather(lines, here, values, meanwhile):
    line = [values] + [lax.ppermute(values, lines.long, shifted(lines.n_long, d)) for d in range(1, lines.n_long)]
    pieces = list(line)
    for d in range(1, lines.n_short):
        pieces += [lax.ppermute(v, lines.short, shifted(lines.n_short, d)) for v in line]
    dims = (lines.outer, lines.inner) + values.shape
    pieces = after(pieces, meanwhile)
    mine = call(
        functools.partial(stack_kernel, lines),
        (1,),
        [pl.BlockSpec(memory_space=pl.ANY)] * len(pieces),
        pl.BlockSpec(dims, lambda *_: (0,) * 4),
        shape(dims, values.dtype),
        0,
        4 * lines.chips * values.size,
        scratch=[pltpu.SemaphoreType.DMA((len(pieces),))],
        scalars=1,
    )(here, *pieces)
    mine = mine.reshape((lines.chips,) + values.shape)
    return mine, lax.ppermute(mine, "c", shifted(2, 1))


def add_first_kernel(here, keep_ref, got_ref, out_ref):
    out_ref[...] = (keep_ref[...].astype(F32) + got_ref[...].astype(F32)).astype(BF)


def add_second_kernel(lines, late, here, keep_ref, got_ref, *refs):
    ins, refs = refs[: lines.n_short - 1], refs[lines.n_short - 1 :]
    late_ref, outs = (refs[0], refs[1:]) if late else (None, refs)
    for k, out in enumerate(outs):
        at = lines.place(lax.rem(here[0] + k, lines.n_long), 0)
        total = keep_ref[at].astype(F32) + got_ref[at].astype(F32)
        for r in ins:
            total = total + r[at].astype(F32)
        if late:
            n = total.shape[1] - SMALL
            out[:, :n] = total[:, :n].astype(BF)
            out[:, n:] = (total[:, n:] + late_ref[at[0] + at[1]]).astype(BF)
        else:
            out[...] = total.astype(BF)


def add_last_kernel(*refs):
    *ins, out = refs
    out[...] = functools.reduce(jnp.add, [r[...].astype(F32) for r in ins]).astype(BF)


class StagedSum:
    def __init__(self, lines, here, keep, send):
        self.lines, self.here = lines, here
        self.got = lines.split(lax.ppermute(send, "c", shifted(2, 1)))
        self.keep = lines.split(keep)
        self.rows, self.columns = keep.shape[1:]
        self.dims = lines.place(lines.n_long, 1) + (self.rows, self.columns)
        self.size = lines.n_long * self.rows * self.columns

    def across(self, d):
        lines = self.lines
        return pl.BlockSpec(self.dims, lambda i, h: lines.place(0, lax.rem(h[1] + d, lines.n_short)) + (0, 0))

    def short(self):
        lines, dims = self.lines, self.dims
        away = [
            call(
                add_first_kernel,
                (1,),
                [self.across(d)] * 2,
                pl.BlockSpec(dims, lambda i, h: (0, 0, 0, 0)),
                shape(dims, BF),
                self.size,
                6 * self.size,
                scalars=1,
            )(self.here, self.keep, self.got)
            for d in range(1, lines.n_short)
        ]
        self.arrived = [lax.ppermute(v, lines.short, shifted(lines.n_short, d + 1)) for d, v in enumerate(away)]
        return away

    def long(self, late=()):
        lines = self.lines
        flat = pl.BlockSpec((self.rows, self.columns), lambda i, h: (0, 0))
        parts = call(
            functools.partial(add_second_kernel, lines, len(late) > 0),
            (1,),
            [self.across(0)] * 2
            + [pl.BlockSpec(self.dims, lambda i, h: (0, 0, 0, 0))] * len(self.arrived)
            + [fixed(*v.shape) for v in late],
            [flat] * lines.n_long,
            [shape((self.rows, self.columns), BF)] * lines.n_long,
            3 * self.size,
            8 * self.size,
            scalars=1,
        )(self.here, self.keep, self.got, *self.arrived, *late)
        self.parts = [parts[0]]
        self.parts += [lax.ppermute(parts[d], lines.long, shifted(lines.n_long, d)) for d in range(1, lines.n_long)]
        return parts

    def last(self):
        return call(
            add_last_kernel,
            (1,),
            [fixed(self.rows, self.columns)] * len(self.parts),
            fixed(self.rows, self.columns),
            shape((self.rows, self.columns), BF),
            self.size,
            3 * self.size,
        )(*self.parts)


def share_kernel(group, here, qkv_ref, up_ref, down_ref, out_ref, *refs):
    *small_refs, att_ref, feed_ref = refs
    side = here[3]
    depth, width = out_ref.shape
    heads = width // group
    for k in range(3):
        parts = [qkv_ref[:, k * width + g * heads : k * width + (g + 1) * heads] for g in range(group)]
        att_ref[:, k * heads : (k + 1) * heads] = pick(parts, side)
    rows = [r[j : j + depth].astype(F32).reshape(1, depth) for r in small_refs for j in range(0, r.shape[0], depth)]
    rows.append(jnp.zeros((SMALL - len(rows), depth), F32))
    att_ref[:, 3 * heads :] = jnp.concatenate(rows, axis=0).T.astype(BF)
    owned = down_ref.shape[0] // group
    hidden = up_ref.shape[1] // group
    for f in range(hidden // owned):
        parts = [up_ref[:, (f * group + g) * owned : (f * group + g + 1) * owned] for g in range(group)]
        feed_ref[:, f * owned : (f + 1) * owned] = pick(parts, side)
    for j in range(owned // depth):
        parts = [down_ref[g * owned + j * depth : g * owned + (j + 1) * depth, :] for g in range(group)]
        feed_ref[:, hidden + j * width : hidden + (j + 1) * width] = pick(parts, side)
    feed_ref[:, 2 * hidden :] = out_ref[...]


def share(here, group, qkv, up, down, out, small):
    depth, width = out.shape
    args = (qkv, up, down, out, *small)
    att, feed_columns = qkv.shape[1] // group + SMALL, 2 * up.shape[1] // group + width
    return call(
        functools.partial(share_kernel, group),
        (1,),
        [fixed(*a.shape) for a in args],
        [fixed(depth, att), fixed(depth, feed_columns)],
        [shape((depth, att), BF), shape((depth, feed_columns), BF)],
        0,
        8 * depth * (att + feed_columns),
        scalars=1,
    )(here, *args)


def finish_attention_kernel(group, here, *refs):
    shares, (out_ref, qkv_ref, *vector_refs) = refs[:group], refs[group:]
    width = out_ref.shape[1]
    heads = width // group
    total = functools.reduce(jnp.add, [r[:, :width].astype(F32) for r in shares])
    out_ref[...] = total
    small = functools.reduce(jnp.add, [r[:, -SMALL:].astype(F32) for r in shares])
    small, row = small.T, 0
    for ref in vector_refs:
        for at in range(0, ref.shape[0], small.shape[1]):
            ref[at : at + small.shape[1]] = small[row]
            row += 1
    for k in range(group):
        source = lax.rem(k - here[3] + group, group)
        for m in range(3):
            at, start = m * width + k * heads, width + m * heads
            parts = [r[:, start : start + heads] for r in shares]
            qkv_ref[:, at : at + heads] = pick(parts, source).astype(F32)


def finish_attention(here, shares, width, counts):
    depth, group = shares[0].shape[0], len(shares)
    return call(
        functools.partial(finish_attention_kernel, group),
        (1,),
        [fixed(*v.shape) for v in shares],
        [fixed(depth, width), fixed(depth, 3 * width)] + [fixed(n * depth) for n in counts],
        [shape((depth, width), F32), shape((depth, 3 * width), F32)] + [shape((n * depth,), F32) for n in counts],
        0,
        24 * depth * width,
        scalars=1,
    )(here, *shares)


def finish_feed_kernel(group, here, *refs):
    shares, (up_ref, down_ref) = refs[:group], refs[group:]
    depth, width = shares[0].shape[0], down_ref.shape[1]
    owned = down_ref.shape[0] // group
    hidden = up_ref.shape[1] // group
    for k in range(group):
        source = lax.rem(k - here[3] + group, group)
        for f in range(hidden // owned):
            at = (f * group + k) * owned
            up_ref[:, at : at + owned] = pick([r[:, f * owned : (f + 1) * owned] for r in shares], source).astype(F32)
        for j in range(owned // depth):
            at, start = k * owned + j * depth, hidden + j * width
            down_ref[at : at + depth, :] = pick([r[:, start : start + width] for r in shares], source).astype(F32)


def finish_feed(here, shares, up_shape, down_shape):
    return call(
        functools.partial(finish_feed_kernel, len(shares)),
        (1,),
        [fixed(*v.shape) for v in shares],
        [fixed(*up_shape), fixed(*down_shape)],
        [shape(up_shape, F32), shape(down_shape, F32)],
        0,
        12 * up_shape[0] * up_shape[1],
        scalars=1,
    )(here, *shares)


def rotated(values, cos, low, high):
    half = 2 * (HD // 3 // 2) // 2
    return values * cos + pltpu.roll(values, values.shape[1] - half, 1) * low + pltpu.roll(values, half, 1) * high


def project_kernel(group, here, *refs):
    clip, refs = refs[:group], refs[group:]
    mine_ref, sib_ref, mine_small, sib_small, cos_ref, low_ref, high_ref, out_ref, w_ref, x_ref, lines_ref, bias = refs
    rows = mine_ref.shape[1]
    core, side, step = here[2], here[3], pl.program_id(0)
    width = out_ref.shape[1]

    @pl.when(step == 0)
    def _():
        owners = []
        for q in range(mine_small.shape[0]):
            a, b = mine_small[q].astype(F32), sib_small[q].astype(F32)
            owners += [jnp.where(core == 0, a, b), jnp.where(core == 0, b, a)]
        lines = jnp.concatenate(owners, axis=0).T[: lines_ref.shape[0]]
        lines_ref[...] = lines
        count = width // rows
        for k in range(3):
            for j in range(count):
                at = [(k * group + g) * count + j for g in range(group)]
                parts = [lines[6 + p % 3 : 7 + p % 3, p // 3 * rows : (p // 3 + 1) * rows] for p in at]
                bias[k : k + 1, j * rows : (j + 1) * rows] = pick(parts, side)
        tokens = clip[0].shape[0]
        block = min(256, tokens)
        for d, ref in enumerate(clip):
            for r in range(0, tokens, block):
                normal, _ = normalise(ref[r : r + block, :].astype(F32))
                at = d * tokens + r
                x_ref[at : at + block, :] = (normal * lines[0:1] + lines[1:2]).astype(BF)

    for q in range(mine_ref.shape[0]):
        w_ref[pl.ds(pl.multiple_of((2 * q + core) * rows, rows), rows), :] = mine_ref[q]
        w_ref[pl.ds(pl.multiple_of((2 * q + 1 - core) * rows, rows), rows), :] = sib_ref[q]
    values = mm(x_ref[...], w_ref[...]) + bias[pl.ds(step, 1), :]

    @pl.when(step < 2)
    def _():
        cos, low, high = cos_ref[...], low_ref[...], high_ref[...]
        for j in range(0, width, 128):
            out_ref[:, j : j + 128] = rotated(values[:, j : j + 128], cos, low, high).astype(BF)

    @pl.when(step >= 2)
    def _():
        out_ref[...] = values.astype(BF)


def project(here, clip, tokens, mine, sib, tables, width):
    depth, group = clip[0].shape[1], len(clip)
    rows = tokens * group
    part = pl.BlockSpec(mine.shape[:2] + (width,), lambda i, h: (0, 0, i))
    small = pl.BlockSpec(mine.shape[:2] + (SMALL,), lambda i, h: (0, 0, 3 * width // SMALL))
    return call(
        functools.partial(project_kernel, group),
        (3,),
        [fixed(tokens, depth)] * group + [part, part, small, small] + [fixed(rows, 128)] * 3,
        [
            pl.BlockSpec((rows, width), lambda i, h: (0, i)),
            pl.BlockSpec((depth, width), lambda i, h: (0, i)),
            fixed(rows, depth),
            fixed(16, depth),
        ],
        [shape((rows, 3 * width), BF), shape((depth, 3 * width), BF), shape((rows, depth), BF), shape((16, depth), F32)],
        6 * rows * depth * width,
        12 * depth * width + 2 * rows * (depth + 3 * width),
        scratch=[pltpu.VMEM((8, width), F32)],
        scalars=1,
    )(here, *clip, mine, sib, mine, sib, *tables)


def rotary_tables(positions):
    width = 2 * (HD // 3 // 2)
    half = width // 2
    freqs = np.power(np.float32(THETA), -(np.arange(half, dtype=np.float32) * np.float32(2.0 / width)))
    column = np.arange(2 * HD) % HD
    turns = column < 3 * width
    axis = np.minimum(column // width, 2)
    freq = np.where(turns, freqs[column % half], 0.0).astype(np.float32)
    leading = turns & (column % width < half)
    trailing = turns & (column % width >= half)
    place = jnp.where(axis == 0, positions[0][:, None], jnp.where(axis == 1, positions[1][:, None], positions[2][:, None]))
    angle = place * freq
    sine = jnp.sin(angle)
    return jnp.cos(angle), jnp.where(leading, -sine, 0.0), jnp.where(trailing, sine, 0.0)


def over_blocks(rows, block, step):
    if rows // block <= 4:
        for i in range(rows // block):
            step(pl.ds(i * block, block))
    else:

        def body(i, carry):
            step(pl.ds(pl.multiple_of(i * block, block), block))
            return carry

        lax.fori_loop(0, rows // block, body, 0)


def attend_kernel(block, q_ref, k_ref, v_ref, o_ref, lse_ref):
    rows = q_ref.shape[0]
    first = lax.broadcasted_iota(jnp.int32, (1, 128), 1) < HD
    masks = (first, jnp.logical_not(first))
    factor = jnp.float32(SCALE * LOG2E)
    zero, one = jnp.zeros((), BF), jnp.ones((), BF)

    def scores_of(rs, h):
        return mm(jnp.where(masks[h], q_ref[rs, :], zero), k_ref[...], NT)

    def finish(scores, h):
        peak = jnp.max(scores, axis=1, keepdims=True) * factor
        weights = jnp.exp2(scores * factor - peak).astype(BF)
        out = mm(weights, jnp.where(masks[h], v_ref[...], one))
        total = out[:, (1 - h) * HD : (1 - h) * HD + 1]
        return out * (1.0 / total), peak + jnp.log2(total)

    def store(rs, left, right):
        o_ref[rs, :] = jnp.where(first, left[0], right[0]).astype(BF)
        lse_ref[rs, :] = jnp.where(first, left[1], right[1])

    if rows // block <= 4:
        places = [pl.ds(i * block, block) for i in range(rows // block)]
        turns = [(rs, h) for rs in places for h in range(2)]
        scores, done = scores_of(*turns[0]), []
        for n, (rs, h) in enumerate(turns):
            ahead = scores_of(*turns[n + 1]) if n + 1 < len(turns) else None
            done.append(finish(scores, h))
            if h == 1:
                store(rs, *done[-2:])
            scores = ahead
    else:
        over_blocks(rows, block, lambda rs: store(rs, *[finish(scores_of(rs, h), h) for h in range(2)]))


def attend_back_kernel(
    block, q_ref, k_ref, v_ref, o_ref, lse_ref, do_ref, cos_ref, low_ref, high_ref, dq_ref, dk_ref, dv_ref, sums_ref, dk_sum, dv_sum
):
    rows = q_ref.shape[0]
    first = lax.broadcasted_iota(jnp.int32, (1, 128), 1) < HD
    masks = (first, jnp.logical_not(first))
    factor = jnp.float32(SCALE * LOG2E)
    zero = jnp.zeros((), BF)
    dk_sum[...] = jnp.zeros_like(dk_sum)
    dv_sum[...] = jnp.zeros_like(dv_sum)

    def step(rs):
        q, do = q_ref[rs, :], do_ref[rs, :]
        od = (o_ref[rs, :].astype(F32) * do.astype(F32)).T
        lse = lse_ref[rs, :].T
        dq = None
        for h, mine in enumerate(masks):
            qh, doh, k = jnp.where(mine, q, zero), jnp.where(mine, do, zero), k_ref[...]
            delta = jnp.sum(od[h * HD : (h + 1) * HD, :], axis=0, keepdims=True)
            p = jnp.exp2(mm(k, qh, NT) * factor - lse[h * HD : h * HD + 1, :])
            ds = (p * (mm(v_ref[...], doh, NT) - delta)).astype(BF)
            dv_sum[...] += mm(p.astype(BF), doh)
            dk_sum[...] += mm(ds, qh)
            part = mm(jnp.where(mine, k, zero), ds, TN)
            dq = part if dq is None else dq + part
        dq = (dq.T * SCALE).astype(BF).astype(F32)
        dq_ref[rs, :] = rotated(dq, cos_ref[rs, :], -low_ref[rs, :], -high_ref[rs, :]).astype(BF)

    over_blocks(rows, block, step)
    dk = (dk_sum[...] * SCALE).astype(BF).astype(F32)
    dk_ref[...] = rotated(dk, cos_ref[...], -low_ref[...], -high_ref[...]).astype(BF)
    dv_ref[...] = dv_sum[...].astype(BF)
    sums = [jnp.sum(r[...].astype(F32), axis=0, keepdims=True) for r in (dq_ref, dk_ref, dv_ref)]
    sums_ref[...] = jnp.concatenate(sums + [jnp.zeros((5, 128), F32)], axis=0)


def pair_spec(rows, first=0):
    return pl.BlockSpec((rows, 128), lambda i: (0, first + i))


def attend(qkv, block=512):
    rows, columns = qkv.shape[0], qkv.shape[1] // 3
    pairs = columns // 128
    return call(
        functools.partial(attend_kernel, min(block, (1 << 19) // rows)),
        (pairs,),
        [pair_spec(rows, k * pairs) for k in range(3)],
        [pair_spec(rows)] * 2,
        [shape((rows, columns), BF), shape((rows, columns), F32)],
        16 * rows * rows * columns,
        rows * columns * 12,
        rows * rows * columns // HD,
    )(qkv, qkv, qkv)


def attend_back(qkv, o, lse, do, tables, block=512):
    rows, columns = o.shape
    pairs = columns // 128
    return call(
        functools.partial(attend_back_kernel, min(block, (1 << 19) // rows)),
        (pairs,),
        [pair_spec(rows, k * pairs) for k in range(3)] + [pair_spec(rows)] * 3 + [fixed(rows, 128)] * 3,
        [pair_spec(rows)] * 3 + [pl.BlockSpec((8, 128), lambda i: (0, i))],
        [shape((rows, columns), BF)] * 3 + [shape((8, columns), F32)],
        40 * rows * rows * columns,
        rows * columns * 20,
        rows * rows * columns // HD,
        [pltpu.VMEM((rows, 128), F32)] * 2,
    )(qkv, qkv, qkv, o, lse, do, *tables)


def normalise(values):
    center = values - jnp.mean(values, axis=-1, keepdims=True)
    factor = lax.rsqrt(jnp.mean(center * center, axis=-1, keepdims=True) + EPS)
    return center * factor, factor


def normalise_back(grads, gain, normal, factor):
    e = grads * gain
    inner = e - jnp.mean(e, axis=-1, keepdims=True) - normal * jnp.mean(e * normal, axis=-1, keepdims=True)
    return factor * inner


def column_sums(out_ref, *parts):
    sums = [jnp.sum(p, axis=0, keepdims=True) for p in parts]
    sums.append(jnp.zeros((8 - len(sums), sums[0].shape[1]), F32))
    block = jnp.concatenate(sums, axis=0)

    @pl.when(pl.program_id(0) == 0)
    def _():
        out_ref[...] = block

    @pl.when(pl.program_id(0) > 0)
    def _():
        out_ref[...] += block


def out_kernel(group, here, *refs):
    atts, weights, (tokens_ref, b_ref, gain_ref, bias_ref, hidden_ref, normed_ref) = (
        refs[:group],
        refs[group : 2 * group],
        refs[2 * group :],
    )
    hidden = tokens_ref[...].astype(F32) + b_ref[...]
    for att, w in zip(atts, weights):
        hidden = hidden + mm(att[...], w[...])
    hidden_ref[...] = hidden
    normed_ref[...] = (normalise(hidden)[0] * gain_ref[...] + bias_ref[...]).astype(BF)


def project_out(here, atts, weight, at, tokens, b, gain, bias, block=256):
    rows, width = tokens.shape
    group, heads = len(atts), atts[0].shape[1]
    row = pl.BlockSpec((block, width), lambda i, h: (i, 0))
    return call(
        functools.partial(out_kernel, group),
        (rows // block,),
        [pl.BlockSpec((block, heads), lambda i, h: (i, 0))] * group
        + [pl.BlockSpec((heads, width), lambda i, h, d=d: (lax.rem(h[3] + d, group), at)) for d in range(group)]
        + [row]
        + [fixed(1, width)] * 3,
        [row, row],
        [shape((rows, width), F32), shape((rows, width), BF)],
        2 * rows * width * width,
        2 * width * width + 10 * rows * width,
        scalars=1,
    )(here, *atts, *[weight] * group, tokens, b, gain, bias)


def hidden_back_kernel(group, here, *refs):
    dn_ref, far_refs, (hidden_ref, og_ref, gain_ref, w_ref, grad_ref, branch_ref, sums_ref, *att_refs) = (
        refs[0],
        refs[1:group],
        refs[group:],
    )
    dn = dn_ref[...]
    for far in far_refs:
        dn = dn + far[...].astype(F32)
    normal, factor = normalise(hidden_ref[...])
    og = og_ref[...].astype(F32)
    grad = og + normalise_back(dn, gain_ref[...], normal, factor)
    grad_ref[...] = grad
    branch = grad.astype(BF)
    branch_ref[...] = branch
    att = mm(branch, w_ref[...], NT).astype(BF)
    heads = att.shape[1] // group
    parts = [att[:, k * heads : (k + 1) * heads] for k in range(group)]
    for d, ref in enumerate(att_refs):
        ref[...] = pick(parts, lax.rem(here[3] + d, group))
    column_sums(sums_ref, dn * normal, dn, branch.astype(F32), og)


def hidden_back(here, dn, dn_far, hidden, og, gain, weight, at, block=256):
    rows, width = hidden.shape
    group = 1 + len(dn_far)
    row = pl.BlockSpec((block, width), lambda i, h: (i, 0))
    share = pl.BlockSpec((block, width // group), lambda i, h: (i, 0))
    return call(
        functools.partial(hidden_back_kernel, group),
        (rows // block,),
        [row] * group + [row, row, fixed(1, width), pl.BlockSpec((width, width), lambda i, h: (0, at))],
        [row, row, fixed(8, width)] + [share] * group,
        [shape((rows, width), F32), shape((rows, width), BF), shape((8, width), F32)]
        + [shape((rows, width // group), BF)] * group,
        2 * rows * width * width,
        2 * width * width + 18 * rows * width,
        scalars=1,
        weight=HIGH,
    )(here, dn, *dn_far, hidden, og, gain, weight)


def tokens_back_kernel(extra, *refs):
    dn_ref, far_refs, (tokens_ref, grad_ref, gain_ref, out_ref) = refs[0], refs[1 : 1 + extra], refs[1 + extra :]
    dn = dn_ref[...]
    for far in far_refs:
        dn = dn + far[...].astype(F32)
    normal, factor = normalise(tokens_ref[...].astype(F32))
    out_ref[...] = grad_ref[...] + normalise_back(dn, gain_ref[...], normal, factor)


def tokens_back(dn, dn_far, tokens, grad, gain, block=256):
    rows, width = tokens.shape
    row = pl.BlockSpec((block, width), lambda i: (i, 0))
    return call(
        functools.partial(tokens_back_kernel, len(dn_far)),
        (rows // block,),
        [row] * (3 + len(dn_far)) + [fixed(1, width)],
        row,
        shape((rows, width), F32),
        20 * rows * width,
        14 * rows * width,
    )(dn, *dn_far, tokens, grad, gain)


def project_back_kernel(dq_ref, dk_ref, dv_ref, w_ref, tokens_ref, out_ref, sums_ref):
    width = dq_ref.shape[1]
    total = functools.reduce(
        jnp.add,
        [mm(g[...], w_ref[:, k * width : (k + 1) * width], NT) for k, g in enumerate((dq_ref, dk_ref, dv_ref))],
    )
    out_ref[...] = total.astype(out_ref.dtype)
    normal, _ = normalise(tokens_ref[...].astype(F32))
    column_sums(sums_ref, total * normal, total)


def project_back(grads, weight, tokens, piece, rows, dtype):
    width, depth = grads[0].shape[1], tokens.shape[1]
    block = rows // 2
    row = pl.BlockSpec((block, depth), lambda i: (i, 0))
    return call(
        project_back_kernel,
        (2,),
        [pl.BlockSpec((block, width), lambda i: (2 * piece + i, 0))] * 3 + [fixed(depth, 3 * width), row],
        [row, fixed(8, depth)],
        [shape((rows, depth), dtype), shape((8, depth), F32)],
        6 * rows * width * depth,
        6 * width * depth + rows * (6 * width + 6 * depth),
    )(*grads, weight, tokens)


def unpack_down(block, rows, width):
    parts = block.shape[1] // width
    if parts == 1:
        return block
    owners = block.shape[0] // rows
    return jnp.concatenate(
        [block[f * rows : (f + 1) * rows, j * width : (j + 1) * width] for f in range(owners) for j in range(parts)], axis=0
    )


def feed_kernel(owned, x_ref, og_ref, up_ref, down_ref, b_ref, act_ref, pre_ref, dn_ref, out_ref, sums_ref, dn_sum, out_sum):
    step, last = pl.program_id(0), pl.num_programs(0) - 1
    width = x_ref.shape[1]
    up = up_ref[...]
    down = unpack_down(down_ref[...], owned, width)
    u = mm(x_ref[...], up) + b_ref[...]
    phi = 0.5 * (1.0 + lax.erf(u * 0.7071067811865476))
    slope = phi + u * jnp.exp(-0.5 * u * u) * 0.3989422804014327
    act = (u * phi).astype(BF)
    act_ref[...] = act
    pre = (mm(og_ref[...], down, NT) * slope).astype(BF)
    pre_ref[...] = pre
    sums_ref[...] = jnp.sum(pre.astype(F32), axis=0, keepdims=True)
    dn = mm(pre, up, NT)
    out = mm(act, down)

    @pl.when(step == 0)
    def _():
        dn_sum[...] = dn
        out_sum[...] = out

    @pl.when(step > 0)
    def _():
        dn_sum[...] += dn
        out_sum[...] += out

    @pl.when(step == last)
    def _():
        dn_ref[...] = dn_sum[...].astype(dn_ref.dtype)
        out_ref[...] = out_sum[...].astype(out_ref.dtype)


def feed(x, og, up, down, packs, bias, owned, dtype, block=512):
    rows, width = x.shape
    hidden = bias.shape[1]
    block = min(block, hidden)
    steps = hidden // block
    down_rows = down.shape[0] // steps
    down_columns = hidden if packs else width
    columns = pl.BlockSpec((rows, block), lambda i: (0, i))
    vector = pl.BlockSpec((1, block), lambda i: (0, i))
    return call(
        functools.partial(feed_kernel, owned),
        (steps,),
        [
            fixed(rows, width),
            fixed(rows, width),
            pl.BlockSpec((width, block), lambda i: (0, i)),
            pl.BlockSpec((down_rows, down_columns), lambda i: (i, int(packs))),
            vector,
        ],
        [columns, columns, fixed(rows, width), fixed(rows, width), vector],
        [
            shape((rows, hidden), BF),
            shape((rows, hidden), BF),
            shape((rows, width), dtype),
            shape((rows, width), dtype),
            shape((1, hidden), F32),
        ],
        8 * rows * width * hidden,
        4 * width * hidden + rows * (4 * hidden + 8 * width),
        2 * rows * hidden,
        [pltpu.VMEM((rows, width), F32)] * 2,
    )(x, og, up, down, bias)


def up_grad_kernel(count, *refs):
    xs, pres, (_, out_ref) = refs[:count], refs[count : 2 * count], refs[2 * count :]
    out_ref[...] = functools.reduce(jnp.add, [mm(x[...], p[...], TN) for x, p in zip(xs, pres)]).astype(BF)


def down_grad_kernel(owned, count, *refs):
    acts, ogs, out_ref = refs[:count], refs[count : 2 * count], refs[2 * count]
    grad = functools.reduce(jnp.add, [mm(a[...], g[...], TN) for a, g in zip(acts, ogs)]).astype(BF)
    width = grad.shape[1]
    parts = out_ref.shape[1] // width
    for f in range(out_ref.shape[0] // owned):
        for j in range(parts):
            start = (f * parts + j) * owned
            out_ref[f * owned : (f + 1) * owned, j * width : (j + 1) * width] = grad[start : start + owned, :]


def down_grad(acts, ogs, owned, block=256):
    count, (rows, hidden), width = len(acts), acts[0].shape, ogs[0].shape[1]
    steps = width // block
    return call(
        functools.partial(down_grad_kernel, owned, count),
        (steps,),
        [pl.BlockSpec((rows, hidden // steps), lambda i: (0, i))] * count + [fixed(rows, width)] * count,
        pl.BlockSpec((block, hidden), lambda i: (i, 1)),
        shape((width, 2 * hidden), BF),
        2 * count * rows * width * hidden,
        2 * count * rows * (width + hidden) + 2 * width * hidden,
    )(*acts, *ogs)


def up_grad(xs, pres, packed, block=256):
    count, (rows, width), hidden = len(xs), xs[0].shape, pres[0].shape[1]
    return pl.pallas_call(
        functools.partial(up_grad_kernel, count),
        grid=(width // block,),
        in_specs=[pl.BlockSpec((rows, block), lambda i: (0, i))] * count
        + [fixed(rows, hidden)] * count
        + [pl.BlockSpec(memory_space=pl.ANY)],
        out_specs=pl.BlockSpec((block, hidden), lambda i: (i, 0)),
        out_shape=shape((width, 2 * hidden), BF),
        input_output_aliases={2 * count: 0},
        compiler_params=pltpu.CompilerParams(vmem_limit_bytes=VMEM_BYTES),
        cost_estimate=pl.CostEstimate(
            flops=2 * count * rows * width * hidden,
            bytes_accessed=2 * count * rows * (width + hidden) + 2 * width * hidden,
            transcendentals=0,
        ),
    )(*xs, *pres, packed)


def deal(here, part, keep_ref, send_ref, at):
    rows, n = keep_ref.shape[1], part.shape[1]
    first = here[2] == 0
    for q in range(keep_ref.shape[0]):
        top, low = part[2 * q * rows : (2 * q + 1) * rows], part[(2 * q + 1) * rows : (2 * q + 2) * rows]
        keep_ref[q, :, at : at + n] = jnp.where(first, top, low)
        send_ref[q, :, at : at + n] = jnp.where(first, low, top)


def out_grad_kernel(group, per_part, here, *refs):
    atts, (branch_ref, keep_ref, send_ref) = refs[:group], refs[group:]
    owner = lax.div(pl.program_id(0), per_part)
    att = pick([a[...] for a in atts], lax.rem(owner - here[3] + group, group))
    deal(here, mm(att, branch_ref[...], TN).astype(BF), keep_ref, send_ref, 0)


def project_out_grad(here, lines, atts, branch, block=256):
    rows, depth = branch.shape
    group = len(atts)
    owned = depth // (2 * lines.chips)
    block = min(block, depth // group)
    per_part = depth // group // block
    out = pl.BlockSpec((block // (2 * owned), owned, depth), lambda i, h: (i, 0, 0))
    return call(
        functools.partial(out_grad_kernel, group, per_part),
        (depth // block,),
        [pl.BlockSpec((rows, block), lambda i, h: (0, lax.rem(i, per_part)))] * group + [fixed(rows, depth)],
        [out, out],
        [shape((lines.chips, owned, depth), BF)] * 2,
        2 * rows * depth * depth,
        2 * depth * (2 * rows + depth),
        scalars=1,
    )(here, *atts, branch)


def project_grad_kernel(here, x_ref, dq_ref, dk_ref, dv_ref, small_ref, keep_ref, send_ref):
    x, at = x_ref[...], 0
    for ref in (dq_ref, dk_ref, dv_ref):
        deal(here, mm(x, ref[...], TN).astype(BF), keep_ref, send_ref, at)
        at += ref.shape[1]
    deal(here, small_ref[...].T.astype(BF), keep_ref, send_ref, at)


def project_grad(here, lines, x, grads, small, block=512):
    rows, depth = x.shape
    width = grads[0].shape[1]
    owned = depth // (2 * lines.chips)
    columns = 3 * width + SMALL
    cols = lambda i, h: (0, i)
    out = pl.BlockSpec((block // (2 * owned), owned, columns), lambda i, h: (i, 0, 0))
    return call(
        project_grad_kernel,
        (depth // block,),
        [pl.BlockSpec((rows, block), cols)] + [fixed(rows, width)] * 3 + [pl.BlockSpec((SMALL, block), cols)],
        [out, out],
        [shape((lines.chips, owned, columns), BF)] * 2,
        6 * rows * depth * width,
        2 * rows * (depth + 3 * width) + 2 * depth * columns,
        scalars=1,
    )(here, x, *grads, small)


def after(values, *earlier):
    return lax.optimization_barrier((values, earlier))[0]


def on_device(
    lines, tokens, positions, ln1_gain, ln1_bias, qkv_weight, qkv_bias, out_weight, out_bias,
    ln2_gain, ln2_bias, fc1_weight, fc1_bias, fc2_weight, fc2_bias, out_grad,
):
    rows, width = tokens.shape[1], tokens.shape[2]
    depth = qkv_weight.shape[0]
    owners, group = width // depth, lax.axis_size(SEQ)
    side, here = lax.axis_index(SEQ), lines.here()
    others = range(1, group)
    heads = width // group
    hidden_owned = fc2_weight.shape[0] // group
    hidden_width = hidden_owned * owners
    packs = hidden_owned % depth == 0

    def gather(values):
        return lax.all_gather(values, SHARD, axis=0, tiled=True)

    def scatter(values):
        return lax.psum_scatter(values, SHARD, scatter_dimension=0, tiled=True)

    def to_next(values, d):
        return lax.ppermute(values, SEQ, shifted(group, d))

    def spread(values):
        return [values] + [to_next(values, d) for d in others]

    def in_order(parts):
        stacked = jnp.stack(parts)
        return [take(stacked, (k - side) % group, 0) for k in range(group)]

    spots = positions[:, 0, :].astype(BF).reshape(-1)
    lines_of = -(-spots.size // width)
    spots = jnp.pad(spots, (0, -(-lines_of // 16) * 16 * width - spots.size)).reshape(-1, width)
    clip = spread(jnp.concatenate([tokens[0], spots], axis=0))
    places = [v[rows:].reshape(-1)[: 3 * rows].reshape(3, rows).astype(F32) for v in clip]
    tables = rotary_tables(jnp.concatenate(places, axis=1))

    names = (ln1_gain, ln1_bias, out_bias, ln2_gain, ln2_bias, fc2_bias, qkv_bias, fc1_bias)
    counts = [p.size // depth for p in names]
    if packs:
        own_att, own_feed = share(here, group, qkv_weight, fc1_weight, fc2_weight, out_weight, names)
        w_up = w_down = w_out = gather(own_feed)
        out_at = 2 * hidden_width // width
    else:
        own_qkv = take(qkv_weight.reshape(depth, 3, group, heads), side, 2).reshape(depth, 3 * heads)
        extra = jnp.concatenate([p.reshape(-1, depth).T for p in names], axis=1)
        own_att = jnp.concatenate([own_qkv, jnp.pad(extra, ((0, 0), (0, SMALL - sum(counts))))], axis=1)
        own_up = take(fc1_weight.reshape(depth, owners, group, hidden_owned), side, 2).reshape(depth, -1)
        own_down = take(fc2_weight.reshape(group, hidden_owned, width), side, 0)
        w_up, w_down, w_out, out_at = gather(own_up), gather(own_down), gather(out_weight), 0
    qkv_mine, qkv_sib = staged_gather(lines, here, own_att, (tables, clip))
    grads = spread(out_grad[0])

    qkv, w_qkv, normed_one, rows_of = project(here, clip, rows, qkv_mine, qkv_sib, tables, heads)
    vectors, at = [], 0
    for n in counts:
        vectors.append(rows_of[at : at + n].reshape(n, owners, depth).transpose(1, 0, 2).reshape(1, -1))
        at += n
    gain_one, _, b_out, gain_two, bias_two, b_down, _, b_up = vectors
    b_up = take(b_up.reshape(owners, group, hidden_owned), side, 1).reshape(1, -1)
    att, lse = attend(qkv)

    att = after(att, grads)
    atts = [att] + [to_next(att[d * rows : (d + 1) * rows], -d) for d in others]
    hidden, normed_two = project_out(here, atts, w_out, out_at, tokens[0], b_out, gain_two, bias_two)
    normed = spread(normed_two)

    fed = [None] * group
    for d in range(group):
        x = after(normed[d], fed[0][2]) if d else normed[0]
        fed[d] = feed(x, grads[d], w_up, w_down, packs, b_up, depth, F32 if d == 0 else BF)
    acts, pres, dns, outs, sums = zip(*fed)
    dn_far = [to_next(dns[d], -d) for d in others]
    out_far = [to_next(outs[d], -d) for d in others]
    dn_own = dns[0]
    if packs:
        fed_grads = down_grad(acts, grads, depth)
        fed_grads = up_grad(normed, pres, fed_grads)
        dn_own = after(dn_own, fed_grads)
    hidden_grad, branch, sums_two, *shares = hidden_back(
        here, dn_own, dn_far, hidden, out_grad[0], gain_two, w_out, out_at
    )
    if packs:
        fed_sum = scatter(fed_grads)
    att_grads = jnp.concatenate([shares[0]] + [to_next(shares[d], d) for d in others], axis=0)

    out_sum = StagedSum(lines, here, *project_out_grad(here, lines, atts, branch))
    att_grads = after(att_grads, out_sum.short())

    *qkv_grads, sums_qkv = attend_back(qkv, att, lse, att_grads, tables)
    qkv_grads = after(qkv_grads, (out_far, out_sum.arrived))

    own = (jnp.arange(group) == side).astype(F32)
    qkv_b = sums_qkv[:3, None, :] * own[None, :, None]
    up_b = functools.reduce(jnp.add, sums).reshape(owners, 1, hidden_owned) * own[None, :, None]
    vectors = (jnp.zeros((2, width), F32), sums_two[2], sums_two[0], sums_two[1], sums_two[3], qkv_b, up_b)
    rows_of = [vectors[0]]
    rows_of += [v.reshape(owners, n, depth).transpose(1, 0, 2).reshape(n, width) for v, n in zip(vectors[1:], counts[2:])]
    rows_of = jnp.pad(jnp.concatenate(rows_of, axis=0), ((0, SMALL - sum(counts)), (0, 0)))
    qkv_sum = StagedSum(lines, here, *project_grad(here, lines, normed_one, qkv_grads, rows_of))

    back = [None] * group
    before = qkv_sum.keep
    for d in list(others) + [0]:
        back[d] = project_back(after(qkv_grads, before), w_qkv, clip[d], d, rows, F32 if d == 0 else BF)
        if d == group - 1:
            qkv_sum.keep = after(qkv_sum.keep, back[d][0])
            before = qkv_sum.short()
    dn_one, sums_one = zip(*back)
    dn_one_far = [to_next(dn_one[d], -d) for d in others]
    sums_one = functools.reduce(jnp.add, sums_one)
    sums_one = sums_one + lax.ppermute(sums_one, "c", shifted(2, 1))
    sums_one = functools.reduce(
        jnp.add, [sums_one] + [lax.ppermute(sums_one, lines.short, shifted(lines.n_short, d)) for d in range(1, lines.n_short)]
    )
    late = sums_one[:2].reshape(2, lines.outer, lines.inner, 2, depth)
    late = take(take(late, here[2], 3), here[1], 2 if lines.outer_long else 1)
    late = jnp.pad(late.transpose(1, 2, 0), ((0, 0), (0, 0), (0, SMALL - 2)))
    out_sum.arrived = after(out_sum.arrived, before)
    out_sum.long()
    qkv_sum.long((late,))
    tokens_grad = tokens_back(dn_one[0], dn_one_far, tokens[0], hidden_grad, gain_one)
    block_out = hidden + outs[0] + b_down
    for far in out_far:
        block_out = block_out + far.astype(F32)
    block_out = block_out.astype(BF)

    def from_next(values):
        return [values] + [to_next(values, -d) for d in others]

    if packs:
        up_total, down_total = finish_feed(here, from_next(fed_sum), fc1_weight.shape, fc2_weight.shape)
    else:
        up_sum = scatter(functools.reduce(jnp.add, [mm(x, p, TN) for x, p in zip(normed, pres)]).astype(BF))
        down_sum = scatter(functools.reduce(jnp.add, [mm(a, g, TN) for a, g in zip(acts, grads)]).astype(BF))
        shares = [v.reshape(depth, owners, hidden_owned) for v in in_order(from_next(up_sum))]
        up_total = jnp.stack(shares, axis=2).reshape(depth, -1).astype(F32)
        down_total = jnp.concatenate(in_order(from_next(down_sum)), axis=0).astype(F32)
    out_last = out_sum.last()
    qkv_sum.parts = after(qkv_sum.parts, (tokens_grad, block_out, up_total, down_total, out_last))
    att_sums = jnp.concatenate([out_last, qkv_sum.last()], axis=1)
    out_total, qkv_total, g1, b1, bo, g2, b2, bd, bq, bu = finish_attention(here, from_next(att_sums), width, counts)
    return (
        block_out[None], tokens_grad[None], g1, b1, qkv_total, bq, out_total, bo, g2, b2, up_total, bu,
        down_total, bd,
    )


def solution(mesh):
    lines = Lines(mesh)
    vector, matrix, tokens = P(SHARD), P(SHARD, None), P(SHARD, SEQ, None)
    return jax.shard_map(
        functools.partial(on_device, lines),
        mesh=lines.mesh,
        in_specs=(
            tokens, P(None, SHARD, SEQ), vector, vector, matrix, vector, matrix, vector, vector, vector, matrix, vector,
            matrix, vector, tokens,
        ),
        out_specs=(
            tokens, tokens, vector, vector, matrix, vector, matrix, vector, vector, vector, matrix, vector, matrix, vector
        ),
        check_vma=False,
    )
```

profile of v0, /device:TPU:0, one launch (start us, length us, event | category | flops | bytes accessed | tf_op | source)
XLA Modules:
  0.0 344.6 jit_solution(3438210937092704719)
XLA Ops:
  7.9 3.3 shard_map.299
  11.4 3.0 collective-permute-start
  14.5 1.6 collective-permute-start.1
  16.1 2.6 collective-permute-start.2
  18.6 1.3 collective-permute-start.3
  20.0 1.5 collective-permute-start.4
  21.5 3.1 collective-permute-done.1.refs_1_
  24.6 1.5 collective-permute-start.5
  26.0 16.1 %collective-permute-done.2.refs_2_ = bf16[64,1664]{1,0:T(8,128)(2,1)S(1)} collective-permute-done((bf16[64,1664]{1,0:T(8,128)(2,1)S(1)}, bf16[64,1664]{1,0:T(8,128)(2,1)S(1)}, u32[]{:S(2)}, u32[]{:S(2)}) %collective-permute-start.2) | collective-permute-done | bytes 213024 | tf_op jit(solution)/shard_map/ppermute | solution.py:124
  42.2 1.5 collective-permute-start.6
  44.3 3.6 %fusion.2 = (f32[1024,128]{1,0:T(8,128)}, f32[1024,128]{1,0:T(8,128)}, f32[1024,128]{1,0:T(8,128)}) fusion(f32[128]{0:T(128)S(1)} %copy-done.40, f32[1024]{0:T(1024)S(1)} %bitcast.58, f32[1024]{0:T(1024)S(1)} %bitcast.57, f32[1024]{0:T(1024)S(1)} %bitcast.56, pred[128]{0:T(512)(128)(4,1)S(1)} %copy-done.41, pred[128]{0:T(512)(128)(4,1)S(1)} %copy-done.42, ...), kind=kLoop, calls=%fused_computation.7 | loop fusion | flops 786432 | bytes 1586176 | tf_op jit(solution)/shard_map/jit(_where)/select_n | solution.py:418
  48.0 2.5 collective-permute-done.6.refs_6_
  50.5 2.4 collective-permute-done.7.refs_7_
  52.9 3.5 %shard_map.300 = bf16[4,2,64,1664]{3,2,1,0:T(8,128)(2,1)} custom-call(s32[4]{0:T(128)} %pad_add_fusion.here, bf16[64,1664]{1,0:T(8,128)(2,1)} %get-tuple-element.99.refs_0_, bf16[64,1664]{1,0:T(8,128)(2,1)} %copy-done.22, bf16[64,1664]{1,0:T(8,128)(2,1)} %copy-done.23, bf16[64,1664]{1,0:T(8,128)(2,1)} %copy-done.24, bf16[64,1664]{1,0:T(8,128)(2,1)} %copy-done.25, ...), custom_call_target="tpu_custom_call" | custom-call | bytes 851968 | tf_op jit(solution)/shard_map/pallas_call | solution.py:130
  57.4 2.9 collective-permute-done.8.refs_3_.refs_5_
  60.3 1.2 copy-done.3
  61.5 13.9 %shard_map.301 = (bf16[1024,1536]{1,0:T(8,128)(2,1)}, bf16[1024,1536]{1,0:T(8,128)(2,1)}, bf16[1024,1024]{1,0:T(8,128)(2,1)}, f32[16,1024]{1,0:T(8,128)}) custom-call(s32[4]{0:T(128)} %pad_add_fusion.here, bf16[528,1024]{1,0:T(8,128)(2,1)} %copy-done, bf16[528,1024]{1,0:T(8,128)(2,1)} %copy-done.4, bf16[8,64,1664]{2,1,0:T(8,128)(2,1)} %bitcast.33, ...), custom_call_target="tpu_custom_call" | custom-call | flops 805306368 | bytes 2883584 | tf_op jit(solution)/shard_map/pallas_call | solution.py:387
  75.5 14.8 %shard_map.302 = (bf16[1024,512]{1,0:T(8,128)(2,1)}, f32[1024,512]{1,0:T(8,128)}) custom-call(bf16[1024,1536]{1,0:T(8,128)(2,1)} %get-tuple-element.107.q_ref.k_ref.v_ref, bf16[1024,1536]{1,0:T(8,128)(2,1)} %get-tuple-element.107.q_ref.k_ref.v_ref, bf16[1024,1536]{1,0:T(8,128)(2,1)} %get-tuple-element.107.q_ref.k_ref.v_ref), custom_call_target="tpu_custom_call" | custom-call | flops 2147483648 | bytes 1572864 | tf_op jit(solution)/shard_map/pallas_call | solution.py:512
  90.3 1.5 slice.63
  91.7 1.4 collective-permute-start.10
  93.8 12.2 %collective-permute-done.10.refs_1_ = bf16[512,512]{1,0:T(8,128)(2,1)S(1)} collective-permute-done((bf16[512,512]{1,0:T(8,128)(2,1)S(1)}, bf16[512,512]{1,0:T(8,128)(2,1)S(1)}, u32[]{:S(2)}, u32[]{:S(2)}) %collective-permute-start.10) | collective-permute-done | bytes 524320 | tf_op jit(solution)/shard_map/ppermute | solution.py:902
  106.0 6.2 %all-gather.2.cloned.1.call-done.refs_2_.refs_3_.up_ref.down_ref.refs_5_ = bf16[1024,5120]{1,0:T(8,128)(2,1)} async-done(((bf16[64,5120]{1,0:T(8,128)(2,1)}), bf16[1024,5120]{1,0:T(8,128)(2,1)}) %all-gather.2.cloned.1.call-update) | async-done | bytes 10485776 | tf_op jit(solution)/shard_map/all_gather | solution.py:896
  112.2 5.6 %shard_map.303 = (f32[512,1024]{1,0:T(8,128)}, bf16[512,1024]{1,0:T(8,128)(2,1)}) custom-call(s32[4]{0:T(128)} %pad_add_fusion.here, bf16[1024,512]{1,0:T(8,128)(2,1)} %get-tuple-element.109.refs_0_.o_ref, bf16[512,512]{1,0:T(8,128)(2,1)} %copy-done.11, bf16[1024,5120]{1,0:T(8,128)(2,1)} %all-gather.2.cloned.1.call-done.refs_2_.refs_3_.up_ref.down_ref.refs_5_, ...), custom_call_target="tpu_custom_call" | custom-call | flops 268435456 | bytes 1835008 | tf_op jit(solution)/shard_map/pallas_call | solution.py:583
  117.8 1.5 collective-permute-start.11
  120.1 16.7 %shard_map.304 = (bf16[512,2048]{1,0:T(8,128)(2,1)}, bf16[512,2048]{1,0:T(8,128)(2,1)}, f32[512,1024]{1,0:T(8,128)}, f32[512,1024]{1,0:T(8,128)}, f32[1,2048]{1,0:T(1,128)}) custom-call(bf16[512,1024]{1,0:T(8,128)(2,1)} %get-tuple-element.113.x_ref.refs_0_, bf16[512,1024]{1,0:T(8,128)(2,1)} %bitcast.46, ...), custom_call_target="tpu_custom_call" | custom-call | flops 2147483648 | bytes 4194304 | tf_op jit(solution)/shard_map/pallas_call | solution.py:740
  136.8 6.5 %collective-permute-done.11.x_ref.refs_1_ = bf16[512,1024]{1,0:T(8,128)(2,1)S(1)} collective-permute-done((bf16[512,1024]{1,0:T(8,128)(2,1)}, bf16[512,1024]{1,0:T(8,128)(2,1)S(1)}, u32[]{:S(2)}, u32[]{:S(2)}) %collective-permute-start.11) | collective-permute-done | bytes 1048608 | tf_op jit(solution)/shard_map/ppermute | solution.py:902
  143.4 1.0 copy-done.8
  144.3 16.0 %shard_map.305 = (bf16[512,2048]{1,0:T(8,128)(2,1)}, bf16[512,2048]{1,0:T(8,128)(2,1)}, bf16[512,1024]{1,0:T(8,128)(2,1)}, bf16[512,1024]{1,0:T(8,128)(2,1)}, f32[1,2048]{1,0:T(1,128)}) custom-call(bf16[512,1024]{1,0:T(8,128)(2,1)} %copy-done.8, bf16[512,1024]{1,0:T(8,128)(2,1)} %copy-done.7, ...), custom_call_target="tpu_custom_call" | custom-call | flops 2147483648 | bytes 4194304 | tf_op jit(solution)/shard_map/pallas_call | solution.py:740
  160.3 1.5 collective-permute-start.13
  161.9 8.4 %shard_map.306.refs_4_ = bf16[1024,4096]{1,0:T(8,128)(2,1)} custom-call(bf16[512,2048]{1,0:T(8,128)(2,1)} %get-tuple-element.121.refs_0_, bf16[512,2048]{1,0:T(8,128)(2,1)} %get-tuple-element.122.refs_1_, bf16[512,1024]{1,0:T(8,128)(2,1)} %bitcast.47, bf16[512,1024]{1,0:T(8,128)(2,1)} %copy-done.7), custom_call_target="tpu_custom_call" | custom-call | flops 1073741824 | bytes 2621440 | tf_op jit(solution)/shard_map/pallas_call | solution.py:784
  170.3 8.7 %shard_map.307 = bf16[1024,4096]{1,0:T(8,128)(2,1)} custom-call(bf16[512,1024]{1,0:T(8,128)(2,1)} %get-tuple-element.113.x_ref.refs_0_, bf16[512,1024]{1,0:T(8,128)(2,1)} %copy-done.8, bf16[512,2048]{1,0:T(8,128)(2,1)} %get-tuple-element.119.refs_2_, bf16[512,2048]{1,0:T(8,128)(2,1)} %get-tuple-element.120.refs_3_, ...), custom_call_target="tpu_custom_call", output_to_operand_aliasing={{}: (4, {})} | custom-call | flops 4294967296 | bytes 10485760 | tf_op jit(solution)/shard_map/pallas_call | solution.py:797
  179.1 6.0 %collective-permute-done.13.refs_1_ = bf16[512,1024]{1,0:T(8,128)(2,1)S(1)} collective-permute-done((bf16[512,1024]{1,0:T(8,128)(2,1)}, bf16[512,1024]{1,0:T(8,128)(2,1)S(1)}, u32[]{:S(2)}, u32[]{:S(2)}) %collective-permute-start.13) | collective-permute-done | bytes 1048608 | tf_op jit(solution)/shard_map/ppermute | solution.py:902
  186.1 8.5 %shard_map.308 = (f32[512,1024]{1,0:T(8,128)}, bf16[512,1024]{1,0:T(8,128)(2,1)}, f32[8,1024]{1,0:T(8,128)}, bf16[512,512]{1,0:T(8,128)(2,1)}, bf16[512,512]{1,0:T(8,128)(2,1)}) custom-call(s32[4]{0:T(128)} %pad_add_fusion.here, f32[512,1024]{1,0:T(8,128)} %get-tuple-element.123.refs_0_, bf16[512,1024]{1,0:T(8,128)(2,1)} %copy-done.45, ...), custom_call_target="tpu_custom_call" | custom-call | flops 214748364800 | bytes 2306867200 | tf_op jit(solution)/shard_map/pallas_call | solution.py:626
  194.6 6.0 %shard_map.309 = (bf16[8,64,1024]{2,1,0:T(8,128)(2,1)}, bf16[8,64,1024]{2,1,0:T(8,128)(2,1)}) custom-call(s32[4]{0:T(128)} %pad_add_fusion.here, bf16[1024,512]{1,0:T(8,128)(2,1)} %get-tuple-element.109.refs_0_.o_ref, bf16[512,512]{1,0:T(8,128)(2,1)} %copy-done.11, bf16[512,1024]{1,0:T(8,128)(2,1)} %get-tuple-element.127.refs_2_), custom_call_target="tpu_custom_call" | custom-call | flops 268435456 | bytes 1048576 | tf_op jit(solution)/shard_map/pallas_call | solution.py:838
  200.6 1.4 collective-permute-start.14
  203.2 12.4 %collective-permute-done.14 = bf16[512,512]{1,0:T(8,128)(2,1)S(1)} collective-permute-done((bf16[512,512]{1,0:T(8,128)(2,1)}, bf16[512,512]{1,0:T(8,128)(2,1)S(1)}, u32[]{:S(2)}, u32[]{:S(2)}) %collective-permute-start.14) | collective-permute-done | bytes 524320 | tf_op jit(solution)/shard_map/ppermute | solution.py:902
  215.6 1.0 pad_maximum_fusion.1.do_ref
  216.7 1.0 copy-done.5
  217.6 2.8 shard_map.310
  220.7 25.3 %shard_map.311 = (bf16[1024,512]{1,0:T(8,128)(2,1)}, bf16[1024,512]{1,0:T(8,128)(2,1)}, bf16[1024,512]{1,0:T(8,128)(2,1)}, f32[8,512]{1,0:T(8,128)}) custom-call(bf16[1024,1536]{1,0:T(8,128)(2,1)} %get-tuple-element.107.q_ref.k_ref.v_ref, bf16[1024,1536]{1,0:T(8,128)(2,1)} %get-tuple-element.107.q_ref.k_ref.v_ref, ...), custom_call_target="tpu_custom_call" | custom-call | flops 5368709120 | bytes 2621440 | tf_op jit(solution)/shard_map/pallas_call | solution.py:527
  248.1 7.9 %shard_map.312 = (bf16[8,64,1664]{2,1,0:T(8,128)(2,1)}, bf16[8,64,1664]{2,1,0:T(8,128)(2,1)}) custom-call(s32[4]{0:T(128)} %pad_add_fusion.here, bf16[1024,1024]{1,0:T(8,128)(2,1)} %get-tuple-element.137.x_ref, bf16[1024,512]{1,0:T(8,128)(2,1)} %get-tuple-element.150.dq_ref, bf16[1024,512]{1,0:T(8,128)(2,1)} %get-tuple-element.151.dk_ref, ...), custom_call_target="tpu_custom_call" | custom-call | flops 805306368 | bytes 2162688 | tf_op jit(solution)/shard_map/pallas_call | solution.py:865
  256.0 5.4 %shard_map.313 = (bf16[512,1024]{1,0:T(8,128)(2,1)}, f32[8,1024]{1,0:T(8,128)}) custom-call(bf16[1024,512]{1,0:T(8,128)(2,1)} %get-tuple-element.150.dq_ref, bf16[1024,512]{1,0:T(8,128)(2,1)} %get-tuple-element.151.dk_ref, bf16[1024,512]{1,0:T(8,128)(2,1)} %get-tuple-element.152.dv_ref, bf16[1024,1536]{1,0:T(8,128)(2,1)} %get-tuple-element.146.w_ref, ...), custom_call_target="tpu_custom_call" | custom-call | flops 402653184 | bytes 1966080 | tf_op jit(solution)/shard_map/pallas_call | solution.py:678
  261.5 1.5 collective-permute-start.18
  262.9 1.2 copy-done.2
  264.1 3.5 %shard_map.314 = bf16[4,1,64,1664]{3,2,1,0:T(8,128)(2,1)} custom-call(s32[4]{0:T(128)} %pad_add_fusion.here, bf16[4,2,64,1664]{3,2,1,0:T(8,128)(2,1)} %bitcast.38, bf16[4,2,64,1664]{3,2,1,0:T(8,128)(2,1)} %bitcast.40), custom_call_target="tpu_custom_call" | custom-call | flops 106496 | bytes 638976 | tf_op jit(solution)/shard_map/pallas_call | solution.py:186
  267.7 1.7 collective-permute-start.22
  269.4 5.6 %shard_map.315 = (f32[512,1024]{1,0:T(8,128)}, f32[8,1024]{1,0:T(8,128)}) custom-call(bf16[1024,512]{1,0:T(8,128)(2,1)} %get-tuple-element.150.dq_ref, bf16[1024,512]{1,0:T(8,128)(2,1)} %get-tuple-element.151.dk_ref, bf16[1024,512]{1,0:T(8,128)(2,1)} %get-tuple-element.152.dv_ref, bf16[1024,1536]{1,0:T(8,128)(2,1)} %get-tuple-element.146.w_ref, ...), custom_call_target="tpu_custom_call" | custom-call | flops 402653184 | bytes 1966080 | tf_op jit(solution)/shard_map/pallas_call | solution.py:678
  275.7 1.2 collective-permute-done.23
  277.2 3.1 shard_map.317
  280.3 2.7 collective-permute-start.19
  283.0 2.2 collective-permute-start.20
  285.2 7.2 %collective-permute-done.24 = f32[8,1024]{1,0:T(8,128)S(1)} collective-permute-done((f32[8,1024]{1,0:T(8,128)S(1)}, f32[8,1024]{1,0:T(8,128)S(1)}, u32[]{:S(2)}, u32[]{:S(2)}) %collective-permute-start.24) | collective-permute-done | bytes 32800 | tf_op jit(solution)/shard_map/ppermute | solution.py:994
  292.4 2.9 reduce-scatter.2.cloned.1.call-done.refs_0_
  295.2 3.2 collective-permute-start.28
  299.5 3.9 %shard_map.319 = (bf16[64,1664]{1,0:T(8,128)(2,1)}, bf16[64,1664]{1,0:T(8,128)(2,1)}, bf16[64,1664]{1,0:T(8,128)(2,1)}, bf16[64,1664]{1,0:T(8,128)(2,1)}) custom-call(s32[4]{0:T(128)} %pad_add_fusion.here, bf16[4,2,64,1664]{3,2,1,0:T(8,128)(2,1)} %bitcast.39, bf16[4,2,64,1664]{3,2,1,0:T(8,128)(2,1)} %bitcast.41, ...), custom_call_target="tpu_custom_call" | custom-call | flops 319488 | bytes 851968 | tf_op jit(solution)/shard_map/pallas_call | solution.py:204
  303.4 1.6 collective-permute-start.25
  305.0 2.4 collective-permute-start.27
  307.5 1.6 add_convert_fusion
  309.1 4.5 %shard_map.316 = f32[512,1024]{1,0:T(8,128)} custom-call(f32[512,1024]{1,0:T(8,128)} %get-tuple-element.153.refs_0_, bf16[512,1024]{1,0:T(8,128)(2,1)} %copy-done.15, bf16[512,1024]{1,0:T(8,128)(2,1)} %bitcast.36, f32[512,1024]{1,0:T(8,128)} %get-tuple-element.154.refs_3_, f32[1,1024]{1,0:T(1,128)} %get-tuple-element.182.refs_4_), custom_call_target="tpu_custom_call" | custom-call | flops 2621440 | bytes 1835008 | tf_op jit(solution)/shard_map/pallas_call | solution.py:652
  314.2 1.8 shard_map.318
  316.9 3.3 shard_map.320
  321.1 2.0 shard_map.321
  324.5 9.6 %collective-permute-done.29.refs_1_ = bf16[64,2688]{1,0:T(8,128)(2,1)S(1)} collective-permute-done((bf16[64,2688]{1,0:T(8,128)(2,1)S(1)}, bf16[64,2688]{1,0:T(8,128)(2,1)S(1)}, u32[]{:S(2)}, u32[]{:S(2)}) %collective-permute-start.29) | collective-permute-done | bytes 344096 | tf_op jit(solution)/shard_map/ppermute | solution.py:902
  334.9 2.9 shard_map.322
  (167 shorter events, 14.8 us)
Async XLA Ops:
  7.2 4.2 %copy-start.1 = (bf16[1,512,1024]{2,1,0:T(8,128)(2,1)S(1)}, bf16[1,512,1024]{2,1,0:T(8,128)(2,1)}, u32[]{:S(2)}) copy-start(bf16[1,512,1024]{2,1,0:T(8,128)(2,1)} %param.20) | copy-start | bytes 3145732
  7.2 105.0 %all-gather.2.cloned.1.call-start = ((), (), s32[]{:S(2)}) async-start(), calls=%async_computation.1 | async-start | bytes 11141120 | tf_op jit(solution)/shard_map/all_gather | solution.py:896
  7.9 36.4 %copy-start.40 = (f32[128]{0:T(128)S(1)}, f32[128]{0:T(128)}, u32[]{:S(2)}) copy-start(f32[128]{0:T(128)} %constant.72.clone) | copy-start | bytes 1540
  7.9 36.4 %copy-start.41 = (pred[128]{0:T(512)(128)(4,1)S(1)}, pred[128]{0:T(512)(128)(4,1)}, u32[]{:S(2)}) copy-start(pred[128]{0:T(512)(128)(4,1)} %constant.74.clone) | copy-start | bytes 388
  7.9 36.4 %copy-start.42 = (pred[128]{0:T(512)(128)(4,1)S(1)}, pred[128]{0:T(512)(128)(4,1)}, u32[]{:S(2)}) copy-start(pred[128]{0:T(512)(128)(4,1)} %constant.70.clone) | copy-start | bytes 388
  7.9 36.4 %copy-start.43 = (pred[128]{0:T(512)(128)(4,1)S(1)}, pred[128]{0:T(512)(128)(4,1)}, u32[]{:S(2)}) copy-start(pred[128]{0:T(512)(128)(4,1)} %constant.71.clone) | copy-start | bytes 388
  7.9 36.4 %copy-start.44 = (pred[128]{0:T(512)(128)(4,1)S(1)}, pred[128]{0:T(512)(128)(4,1)}, u32[]{:S(2)}) copy-start(pred[128]{0:T(512)(128)(4,1)} %constant.73.clone) | copy-start | bytes 388
  11.2 284.1 %reduce-scatter.2.cloned.1.call-start = ((), (), s32[]{:S(2)}) async-start(), calls=%async_computation.2 | async-start | bytes 8912896 | tf_op jit(solution)/shard_map/reduce_scatter | solution.py:899
  11.4 45.0 %copy-start = (bf16[528,1024]{1,0:T(8,128)(2,1)}, bf16[528,1024]{1,0:T(8,128)(2,1)S(1)}, u32[]{:S(2)}) copy-start(bf16[528,1024]{1,0:T(8,128)(2,1)S(1)} %pad_maximum_fusion.refs_0_.tokens_ref) | copy-start | bytes 3244036
  11.4 32.8 %collective-permute-start = (bf16[528,1024]{1,0:T(8,128)(2,1)S(1)}, bf16[528,1024]{1,0:T(8,128)(2,1)S(1)}, u32[]{:S(2)}, u32[]{:S(2)}) collective-permute-start(bf16[528,1024]{1,0:T(8,128)(2,1)S(1)} %pad_maximum_fusion.refs_0_.tokens_ref), channel_id=1, source_target_pairs={{0,1},{1,0},{2,3},{3,2},{4,5},{5,4},{6,7},{7,6},{8,9},{9,8},{10,11... | collective-permute-start | bytes 3244040 | tf_op jit(solution)/shard_map/ppermute | solution.py:902
  14.5 10.1 %collective-permute-start.1 = (bf16[64,1664]{1,0:T(8,128)(2,1)S(1)}, bf16[64,1664]{1,0:T(8,128)(2,1)S(1)}, u32[]{:S(2)}, u32[]{:S(2)}) collective-permute-start(bf16[64,1664]{1,0:T(8,128)(2,1)S(1)} %copy-done.21), channel_id=1, source_target_pairs={{0,8},{8,16},{16,24},{24,0},{1,9},{9,17},{17,25},{25,1},{2,10},{10... | collective-permute-start | bytes 638984 | tf_op jit(solution)/shard_map/ppermute | solution.py:124
  16.1 26.1 %collective-permute-start.2 = (bf16[64,1664]{1,0:T(8,128)(2,1)S(1)}, bf16[64,1664]{1,0:T(8,128)(2,1)S(1)}, u32[]{:S(2)}, u32[]{:S(2)}) collective-permute-start(bf16[64,1664]{1,0:T(8,128)(2,1)S(1)} %copy-done.21), channel_id=1, source_target_pairs={{0,16},{8,24},{16,0},{24,8},{1,17},{9,25},{17,1},{25,9},{2,18},{10... | collective-permute-start | bytes 638984 | tf_op jit(solution)/shard_map/ppermute | solution.py:124
  18.6 25.0 %collective-permute-start.3 = (bf16[64,1664]{1,0:T(8,128)(2,1)S(1)}, bf16[64,1664]{1,0:T(8,128)(2,1)S(1)}, u32[]{:S(2)}, u32[]{:S(2)}) collective-permute-start(bf16[64,1664]{1,0:T(8,128)(2,1)S(1)} %copy-done.21), channel_id=1, source_target_pairs={{0,24},{8,0},{16,8},{24,16},{1,25},{9,1},{17,9},{25,17},{2,26},{10... | collective-permute-start | bytes 638984 | tf_op jit(solution)/shard_map/ppermute | solution.py:124
  20.0 27.9 %collective-permute-start.4 = (bf16[64,1664]{1,0:T(8,128)(2,1)S(1)}, bf16[64,1664]{1,0:T(8,128)(2,1)S(1)}, u32[]{:S(2)}, u32[]{:S(2)}) collective-permute-start(bf16[64,1664]{1,0:T(8,128)(2,1)S(1)} %copy-done.21), channel_id=1, source_target_pairs={{0,4},{4,0},{1,5},{5,1},{2,6},{6,2},{3,7},{7,3},{8,12},{12,8},{9,1... | collective-permute-start | bytes 638984 | tf_op jit(solution)/shard_map/ppermute | solution.py:127
  24.5 28.3 %copy-start.22 = (bf16[64,1664]{1,0:T(8,128)(2,1)}, bf16[64,1664]{1,0:T(8,128)(2,1)S(1)}, u32[]{:S(2)}) copy-start(bf16[64,1664]{1,0:T(8,128)(2,1)S(1)} %collective-permute-done.1.refs_1_) | copy-start | bytes 638980
  24.6 23.4 %collective-permute-start.5 = (bf16[64,1664]{1,0:T(8,128)(2,1)S(1)}, bf16[64,1664]{1,0:T(8,128)(2,1)S(1)}, u32[]{:S(2)}, u32[]{:S(2)}) collective-permute-start(bf16[64,1664]{1,0:T(8,128)(2,1)S(1)} %collective-permute-done.1.refs_1_), channel_id=1, source_target_pairs={{0,4},{4,0},{1,5},{5,1},{2,6},{6,2},{3,7},{7,3},{8,12},{12,8},{9,1... | collective-permute-start | bytes 638984 | tf_op jit(solution)/shard_map/ppermute | solution.py:127
  42.2 10.7 %copy-start.23 = (bf16[64,1664]{1,0:T(8,128)(2,1)}, bf16[64,1664]{1,0:T(8,128)(2,1)S(1)}, u32[]{:S(2)}) copy-start(bf16[64,1664]{1,0:T(8,128)(2,1)S(1)} %collective-permute-done.2.refs_2_) | copy-start | bytes 638980
  42.2 8.3 %collective-permute-start.6 = (bf16[64,1664]{1,0:T(8,128)(2,1)S(1)}, bf16[64,1664]{1,0:T(8,128)(2,1)}, u32[]{:S(2)}, u32[]{:S(2)}) collective-permute-start(bf16[64,1664]{1,0:T(8,128)(2,1)S(1)} %collective-permute-done.2.refs_2_), channel_id=1, source_target_pairs={{0,4},{4,0},{1,5},{5,1},{2,6},{6,2},{3,7},{7,3},{8,12},{12,8},{9,1... | collective-permute-start | bytes 638984 | tf_op jit(solution)/shard_map/ppermute | solution.py:127
  43.7 9.2 %copy-start.24 = (bf16[64,1664]{1,0:T(8,128)(2,1)}, bf16[64,1664]{1,0:T(8,128)(2,1)S(1)}, u32[]{:S(2)}) copy-start(bf16[64,1664]{1,0:T(8,128)(2,1)S(1)} %collective-permute-done.3.refs_3_) | copy-start | bytes 638980
  43.7 9.2 %collective-permute-start.7 = (bf16[64,1664]{1,0:T(8,128)(2,1)S(1)}, bf16[64,1664]{1,0:T(8,128)(2,1)}, u32[]{:S(2)}, u32[]{:S(2)}) collective-permute-start(bf16[64,1664]{1,0:T(8,128)(2,1)S(1)} %collective-permute-done.3.refs_3_), channel_id=1, source_target_pairs={{0,4},{4,0},{1,5},{5,1},{2,6},{6,2},{3,7},{7,3},{8,12},{12,8},{9,1... | collective-permute-start | bytes 638984 | tf_op jit(solution)/shard_map/ppermute | solution.py:127
  44.2 12.2 %copy-start.4 = (bf16[528,1024]{1,0:T(8,128)(2,1)}, bf16[528,1024]{1,0:T(8,128)(2,1)S(1)}, u32[]{:S(2)}) copy-start(bf16[528,1024]{1,0:T(8,128)(2,1)S(1)} %collective-permute-done.refs_1_.tokens_ref) | copy-start | bytes 3244036
  47.9 8.6 %copy-start.6 = (bf16[1,512,1024]{2,1,0:T(8,128)(2,1)S(1)}, bf16[1,512,1024]{2,1,0:T(8,128)(2,1)}, u32[]{:S(2)}) copy-start(bf16[1,512,1024]{2,1,0:T(8,128)(2,1)} %param.34) | copy-start | bytes 3145732
  47.9 5.0 %copy-start.25 = (bf16[64,1664]{1,0:T(8,128)(2,1)}, bf16[64,1664]{1,0:T(8,128)(2,1)S(1)}, u32[]{:S(2)}) copy-start(bf16[64,1664]{1,0:T(8,128)(2,1)S(1)} %collective-permute-done.4.refs_4_) | copy-start | bytes 638980
  47.9 5.0 %copy-start.26 = (bf16[64,1664]{1,0:T(8,128)(2,1)}, bf16[64,1664]{1,0:T(8,128)(2,1)S(1)}, u32[]{:S(2)}) copy-start(bf16[64,1664]{1,0:T(8,128)(2,1)S(1)} %collective-permute-done.5.refs_5_) | copy-start | bytes 638980
  56.5 3.9 %collective-permute-start.8 = (bf16[8,64,1664]{2,1,0:T(8,128)(2,1)}, bf16[8,64,1664]{2,1,0:T(8,128)(2,1)S(1)}, u32[]{:S(2)}, u32[]{:S(2)}) collective-permute-start(bf16[8,64,1664]{2,1,0:T(8,128)(2,1)} %bitcast.32), channel_id=1, source_target_pairs={{0,2},{2,0},{1,3},{3,1},{4,6},{6,4},{5,7},{7,5},{8,10},{10,8},{9,1... | collective-permute-start | bytes 5111816 | tf_op jit(solution)/shard_map/ppermute | solution.py:142
  56.5 33.7 %collective-permute-start.9 = (bf16[512,1024]{1,0:T(8,128)(2,1)S(1)}, bf16[512,1024]{1,0:T(8,128)(2,1)S(1)}, u32[]{:S(2)}, u32[]{:S(2)}) collective-permute-start(bf16[512,1024]{1,0:T(8,128)(2,1)S(1)} %bitcast.49), channel_id=1, source_target_pairs={{0,1},{1,0},{2,3},{3,2},{4,5},{5,4},{6,7},{7,6},{8,9},{9,8},{10,11... | collective-permute-start | bytes 3145736 | tf_op jit(solution)/shard_map/ppermute | solution.py:902
  75.5 17.7 %copy-start.35 = (f32[16,1024]{1,0:T(8,128)S(1)}, f32[16,1024]{1,0:T(8,128)}, u32[]{:S(2)}) copy-start(f32[16,1024]{1,0:T(8,128)} %get-tuple-element.111) | copy-start | bytes 196612
  90.3 27.5 %copy-start.7 = (bf16[512,1024]{1,0:T(8,128)(2,1)}, bf16[512,1024]{1,0:T(8,128)(2,1)S(1)}, u32[]{:S(2)}) copy-start(bf16[512,1024]{1,0:T(8,128)(2,1)S(1)} %collective-permute-done.9.og_ref.refs_3_) | copy-start | bytes 3145732
  91.7 14.2 %collective-permute-start.10 = (bf16[512,512]{1,0:T(8,128)(2,1)S(1)}, bf16[512,512]{1,0:T(8,128)(2,1)S(1)}, u32[]{:S(2)}, u32[]{:S(2)}) collective-permute-start(bf16[512,512]{1,0:T(8,128)(2,1)S(1)} %slice.63), channel_id=1, source_target_pairs={{0,1},{1,0},{2,3},{3,2},{4,5},{5,4},{6,7},{7,6},{8,9},{9,8},{10,11... | collective-permute-start | bytes 1572872 | tf_op jit(solution)/shard_map/ppermute | solution.py:902
  106.0 6.2 %copy-start.11 = (bf16[512,512]{1,0:T(8,128)(2,1)}, bf16[512,512]{1,0:T(8,128)(2,1)S(1)}, u32[]{:S(2)}) copy-start(bf16[512,512]{1,0:T(8,128)(2,1)S(1)} %collective-permute-done.10.refs_1_) | copy-start | bytes 1572868
  117.8 25.6 %collective-permute-start.11 = (bf16[512,1024]{1,0:T(8,128)(2,1)}, bf16[512,1024]{1,0:T(8,128)(2,1)S(1)}, u32[]{:S(2)}, u32[]{:S(2)}) collective-permute-start(bf16[512,1024]{1,0:T(8,128)(2,1)} %get-tuple-element.113.x_ref.refs_0_), channel_id=1, source_target_pairs={{0,1},{1,0},{2,3},{3,2},{4,5},{5,4},{6,7},{7,6},{8,9},{9,8},{10,11... | collective-permute-start | bytes 3145736 | tf_op jit(solution)/shard_map/ppermute | solution.py:902
  160.3 24.8 %collective-permute-start.13 = (bf16[512,1024]{1,0:T(8,128)(2,1)}, bf16[512,1024]{1,0:T(8,128)(2,1)S(1)}, u32[]{:S(2)}, u32[]{:S(2)}) collective-permute-start(bf16[512,1024]{1,0:T(8,128)(2,1)} %get-tuple-element.124), channel_id=1, source_target_pairs={{0,1},{1,0},{2,3},{3,2},{4,5},{5,4},{6,7},{7,6},{8,9},{9,8},{10,11... | collective-permute-start | bytes 3145736 | tf_op jit(solution)/shard_map/ppermute | solution.py:902
  194.6 8.3 %copy-start.37 = (f32[1,2048]{1,0:T(1,128)S(1)}, f32[1,2048]{1,0:T(1,128)}, u32[]{:S(2)}) copy-start(f32[1,2048]{1,0:T(1,128)} %get-tuple-element.140) | copy-start | bytes 24580
  194.6 8.3 %copy-start.38 = (f32[1,2048]{1,0:T(1,128)S(1)}, f32[1,2048]{1,0:T(1,128)}, u32[]{:S(2)}) copy-start(f32[1,2048]{1,0:T(1,128)} %get-tuple-element.141) | copy-start | bytes 24580
  194.6 8.6 %copy-start.39 = (f32[8,1024]{1,0:T(8,128)S(1)}, f32[8,1024]{1,0:T(8,128)}, u32[]{:S(2)}) copy-start(f32[8,1024]{1,0:T(8,128)} %get-tuple-element.138) | copy-start | bytes 98308
  194.6 21.0 %copy-start.19 = (bf16[512,512]{1,0:T(8,128)(2,1)S(1)}, bf16[512,512]{1,0:T(8,128)(2,1)}, u32[]{:S(2)}) copy-start(bf16[512,512]{1,0:T(8,128)(2,1)} %get-tuple-element.125) | copy-start | bytes 1572868
  200.6 16.0 %collective-permute-start.15 = (bf16[8,64,1024]{2,1,0:T(8,128)(2,1)}, bf16[8,64,1024]{2,1,0:T(8,128)(2,1)S(1)}, u32[]{:S(2)}, u32[]{:S(2)}) collective-permute-start(bf16[8,64,1024]{2,1,0:T(8,128)(2,1)} %get-tuple-element.129), channel_id=1, source_target_pairs={{0,2},{2,0},{1,3},{3,1},{4,6},{6,4},{5,7},{7,5},{8,10},{10,8},{9,1... | collective-permute-start | bytes 3145736 | tf_op jit(solution)/shard_map/ppermute | solution.py:173
  200.6 15.0 %collective-permute-start.14 = (bf16[512,512]{1,0:T(8,128)(2,1)}, bf16[512,512]{1,0:T(8,128)(2,1)S(1)}, u32[]{:S(2)}, u32[]{:S(2)}) collective-permute-start(bf16[512,512]{1,0:T(8,128)(2,1)} %get-tuple-element.126), channel_id=1, source_target_pairs={{0,1},{1,0},{2,3},{3,2},{4,5},{5,4},{6,7},{7,6},{8,9},{9,8},{10,11... | collective-permute-start | bytes 1572872 | tf_op jit(solution)/shard_map/ppermute | solution.py:902
  202.2 45.8 %collective-permute-start.12 = (bf16[512,1024]{1,0:T(8,128)(2,1)}, bf16[512,1024]{1,0:T(8,128)(2,1)S(1)}, u32[]{:S(2)}, u32[]{:S(2)}) collective-permute-start(bf16[512,1024]{1,0:T(8,128)(2,1)} %get-tuple-element.117), channel_id=1, source_target_pairs={{0,1},{1,0},{2,3},{3,2},{4,5},{5,4},{6,7},{7,6},{8,9},{9,8},{10,11... | collective-permute-start | bytes 3145736 | tf_op jit(solution)/shard_map/ppermute | solution.py:902
  220.5 27.6 %collective-permute-start.16 = (bf16[4,1,64,1024]{3,2,1,0:T(8,128)(2,1)}, bf16[4,1,64,1024]{3,2,1,0:T(8,128)(2,1)S(1)}, u32[]{:S(2)}, u32[]{:S(2)}) collective-permute-start(bf16[4,1,64,1024]{3,2,1,0:T(8,128)(2,1)} %shard_map.310), channel_id=1, source_target_pairs={{0,4},{4,0},{1,5},{5,1},{2,6},{6,2},{3,7},{7,3},{8,12},{12,8},{9,1... | collective-permute-start | bytes 1572872 | tf_op jit(solution)/shard_map/ppermute | solution.py:198
  248.1 7.9 %copy-start.13 = (bf16[512,1024]{1,0:T(8,128)(2,1)}, bf16[512,1024]{1,0:T(8,128)(2,1)S(1)}, u32[]{:S(2)}) copy-start(bf16[512,1024]{1,0:T(8,128)(2,1)S(1)} %collective-permute-done.12) | copy-start | bytes 3145732
  248.1 7.9 %copy-start.18 = (bf16[4,1,64,1024]{3,2,1,0:T(8,128)(2,1)}, bf16[4,1,64,1024]{3,2,1,0:T(8,128)(2,1)S(1)}, u32[]{:S(2)}) copy-start(bf16[4,1,64,1024]{3,2,1,0:T(8,128)(2,1)S(1)} %collective-permute-done.16.refs_0_) | copy-start | bytes 1572868
  256.0 7.0 %collective-permute-start.17 = (bf16[8,64,1664]{2,1,0:T(8,128)(2,1)}, bf16[8,64,1664]{2,1,0:T(8,128)(2,1)S(1)}, u32[]{:S(2)}, u32[]{:S(2)}) collective-permute-start(bf16[8,64,1664]{2,1,0:T(8,128)(2,1)} %get-tuple-element.149), channel_id=1, source_target_pairs={{0,2},{2,0},{1,3},{3,1},{4,6},{6,4},{5,7},{7,5},{8,10},{10,8},{9,1... | collective-permute-start | bytes 5111816 | tf_op jit(solution)/shard_map/ppermute | solution.py:173
  261.5 41.9 %collective-permute-start.18 = (bf16[512,1024]{1,0:T(8,128)(2,1)}, bf16[512,1024]{1,0:T(8,128)(2,1)S(1)}, u32[]{:S(2)}, u32[]{:S(2)}) collective-permute-start(bf16[512,1024]{1,0:T(8,128)(2,1)} %get-tuple-element.147), channel_id=1, source_target_pairs={{0,1},{1,0},{2,3},{3,2},{4,5},{5,4},{6,7},{7,6},{8,9},{9,8},{10,11... | collective-permute-start | bytes 3145736 | tf_op jit(solution)/shard_map/ppermute | solution.py:902
  267.6 7.3 %copy-start.33 = (f32[8,1024]{1,0:T(8,128)S(1)}, f32[8,1024]{1,0:T(8,128)}, u32[]{:S(2)}) copy-start(f32[8,1024]{1,0:T(8,128)} %get-tuple-element.161) | copy-start | bytes 98308
  267.7 31.7 %collective-permute-start.22 = (bf16[4,1,64,1664]{3,2,1,0:T(8,128)(2,1)}, bf16[4,1,64,1664]{3,2,1,0:T(8,128)(2,1)}, u32[]{:S(2)}, u32[]{:S(2)}) collective-permute-start(bf16[4,1,64,1664]{3,2,1,0:T(8,128)(2,1)} %shard_map.314), channel_id=1, source_target_pairs={{0,4},{4,0},{1,5},{5,1},{2,6},{6,2},{3,7},{7,3},{8,12},{12,8},{9,1... | collective-permute-start | bytes 2555912 | tf_op jit(solution)/shard_map/ppermute | solution.py:198
  275.7 1.2 collective-permute-start.23
  276.9 15.5 %collective-permute-start.24 = (f32[8,1024]{1,0:T(8,128)S(1)}, f32[8,1024]{1,0:T(8,128)S(1)}, u32[]{:S(2)}, u32[]{:S(2)}) collective-permute-start(f32[8,1024]{1,0:T(8,128)S(1)} %add.61), channel_id=1, source_target_pairs={{0,4},{4,0},{1,5},{5,1},{2,6},{6,2},{3,7},{7,3},{8,12},{12,8},{9,1... | collective-permute-start | bytes 98312 | tf_op jit(solution)/shard_map/ppermute | solution.py:994
  277.2 30.2 %copy-start.14 = (bf16[512,1024]{1,0:T(8,128)(2,1)S(1)}, bf16[512,1024]{1,0:T(8,128)(2,1)}, u32[]{:S(2)}) copy-start(bf16[512,1024]{1,0:T(8,128)(2,1)} %copy-done.13) | copy-start | bytes 3145732
  280.3 24.7 %collective-permute-start.19 = (bf16[64,1024]{1,0:T(8,128)(2,1)}, bf16[64,1024]{1,0:T(8,128)(2,1)S(1)}, u32[]{:S(2)}, u32[]{:S(2)}) collective-permute-start(bf16[64,1024]{1,0:T(8,128)(2,1)} %get-tuple-element.157), channel_id=1, source_target_pairs={{0,8},{8,16},{16,24},{24,0},{1,9},{9,17},{17,25},{25,1},{2,10},{10... | collective-permute-start | bytes 393224 | tf_op jit(solution)/shard_map/ppermute | solution.py:217
  283.0 22.0 %collective-permute-start.20 = (bf16[64,1024]{1,0:T(8,128)(2,1)}, bf16[64,1024]{1,0:T(8,128)(2,1)S(1)}, u32[]{:S(2)}, u32[]{:S(2)}) collective-permute-start(bf16[64,1024]{1,0:T(8,128)(2,1)} %get-tuple-element.158), channel_id=1, source_target_pairs={{0,16},{8,24},{16,0},{24,8},{1,17},{9,25},{17,1},{25,9},{2,18},{10... | collective-permute-start | bytes 393224 | tf_op jit(solution)/shard_map/ppermute | solution.py:217
  295.2 20.8 %collective-permute-start.28 = (bf16[64,4096]{1,0:T(8,128)(2,1)}, bf16[64,4096]{1,0:T(8,128)(2,1)S(1)}, u32[]{:S(2)}, u32[]{:S(2)}) collective-permute-start(bf16[64,4096]{1,0:T(8,128)(2,1)} %reduce-scatter.2.cloned.1.call-done.refs_0_), channel_id=1, source_target_pairs={{0,1},{1,0},{2,3},{3,2},{4,5},{5,4},{6,7},{7,6},{8,9},{9,8},{10,11... | collective-permute-start | bytes 1572872 | tf_op jit(solution)/shard_map/ppermute | solution.py:902
  299.4 8.1 %copy-start.9 = (f32[512,1024]{1,0:T(8,128)S(1)}, f32[512,1024]{1,0:T(8,128)}, u32[]{:S(2)}) copy-start(f32[512,1024]{1,0:T(8,128)} %get-tuple-element.112.refs_2_) | copy-start | bytes 6291460
  299.4 8.1 %copy-start.10 = (f32[512,1024]{1,0:T(8,128)S(1)}, f32[512,1024]{1,0:T(8,128)}, u32[]{:S(2)}) copy-start(f32[512,1024]{1,0:T(8,128)} %get-tuple-element.114) | copy-start | bytes 6291460
  299.4 8.1 %copy-start.36 = (f32[1,1024]{1,0:T(1,128)S(1)}, f32[1,1024]{1,0:T(1,128)}, u32[]{:S(2)}) copy-start(f32[1,1024]{1,0:T(1,128)} %get-tuple-element.183) | copy-start | bytes 12292
  299.4 14.2 %collective-permute-start.21 = (bf16[64,1024]{1,0:T(8,128)(2,1)}, bf16[64,1024]{1,0:T(8,128)(2,1)S(1)}, u32[]{:S(2)}, u32[]{:S(2)}) collective-permute-start(bf16[64,1024]{1,0:T(8,128)(2,1)} %get-tuple-element.159), channel_id=1, source_target_pairs={{0,24},{8,0},{16,8},{24,16},{1,25},{9,1},{17,9},{25,17},{2,26},{10... | collective-permute-start | bytes 393224 | tf_op jit(solution)/shard_map/ppermute | solution.py:217
  303.4 5.7 %copy-start.15 = (bf16[512,1024]{1,0:T(8,128)(2,1)}, bf16[512,1024]{1,0:T(8,128)(2,1)S(1)}, u32[]{:S(2)}) copy-start(bf16[512,1024]{1,0:T(8,128)(2,1)S(1)} %collective-permute-done.18.refs_1_) | copy-start | bytes 3145732
  303.4 16.8 %collective-permute-start.25 = (bf16[64,1664]{1,0:T(8,128)(2,1)}, bf16[64,1664]{1,0:T(8,128)(2,1)S(1)}, u32[]{:S(2)}, u32[]{:S(2)}) collective-permute-start(bf16[64,1664]{1,0:T(8,128)(2,1)} %get-tuple-element.163), channel_id=1, source_target_pairs={{0,8},{8,16},{16,24},{24,0},{1,9},{9,17},{17,25},{25,1},{2,10},{10... | collective-permute-start | bytes 638984 | tf_op jit(solution)/shard_map/ppermute | solution.py:217
  305.0 4.1 %copy-start.30 = (bf16[64,1024]{1,0:T(8,128)(2,1)}, bf16[64,1024]{1,0:T(8,128)(2,1)S(1)}, u32[]{:S(2)}) copy-start(bf16[64,1024]{1,0:T(8,128)(2,1)S(1)} %collective-permute-done.19.refs_1_) | copy-start | bytes 393220
  305.0 15.4 %collective-permute-start.26 = (bf16[64,1664]{1,0:T(8,128)(2,1)}, bf16[64,1664]{1,0:T(8,128)(2,1)S(1)}, u32[]{:S(2)}, u32[]{:S(2)}) collective-permute-start(bf16[64,1664]{1,0:T(8,128)(2,1)} %get-tuple-element.164), channel_id=1, source_target_pairs={{0,16},{8,24},{16,0},{24,8},{1,17},{9,25},{17,1},{25,9},{2,18},{10... | collective-permute-start | bytes 638984 | tf_op jit(solution)/shard_map/ppermute | solution.py:217
  305.0 15.4 %collective-permute-start.27 = (bf16[64,1664]{1,0:T(8,128)(2,1)}, bf16[64,1664]{1,0:T(8,128)(2,1)S(1)}, u32[]{:S(2)}, u32[]{:S(2)}) collective-permute-start(bf16[64,1664]{1,0:T(8,128)(2,1)} %get-tuple-element.165), channel_id=1, source_target_pairs={{0,24},{8,0},{16,8},{24,16},{1,25},{9,1},{17,9},{25,17},{2,26},{10... | collective-permute-start | bytes 638984 | tf_op jit(solution)/shard_map/ppermute | solution.py:217
  316.1 7.1 %copy-start.16 = (bf16[64,1024]{1,0:T(8,128)(2,1)S(1)}, bf16[64,1024]{1,0:T(8,128)(2,1)}, u32[]{:S(2)}) copy-start(bf16[64,1024]{1,0:T(8,128)(2,1)} %shard_map.318) | copy-start | bytes 393220
  324.1 10.0 %copy-start.12 = (bf16[64,2688]{1,0:T(8,128)(2,1)}, bf16[64,2688]{1,0:T(8,128)(2,1)S(1)}, u32[]{:S(2)}) copy-start(bf16[64,2688]{1,0:T(8,128)(2,1)S(1)} %pad_maximum_fusion.2.refs_0_) | copy-start | bytes 1032196
  324.1 10.0 %collective-permute-start.29 = (bf16[64,2688]{1,0:T(8,128)(2,1)S(1)}, bf16[64,2688]{1,0:T(8,128)(2,1)S(1)}, u32[]{:S(2)}, u32[]{:S(2)}) collective-permute-start(bf16[64,2688]{1,0:T(8,128)(2,1)S(1)} %pad_maximum_fusion.2.refs_0_), channel_id=1, source_target_pairs={{0,1},{1,0},{2,3},{3,2},{4,5},{5,4},{6,7},{7,6},{8,9},{9,8},{10,11... | collective-permute-start | bytes 1032200 | tf_op jit(solution)/shard_map/ppermute | solution.py:902
  (14 other events, 21.0 us)
Sparse Core Ops, SparseCore 0:
  11.3 100.8 all-gather.1
  179.2 115.9 reduce-scatter.1
where the time goes:
time: 348 us; the launch traced here: 345 us
  Pallas kernels  178 us (51%)
  waiting for transfers between devices  91.5 us (26%)
  starting transfers between devices  37.5 us (11%)
  local copies, waits for them, and re-layouts  14.5 us (4%)
  between operations  14.5 us (4%)
  other arithmetic  8.84 us (3%)
    ppermute x10, waiting for transfers between devices, to_next(): return lax.ppermute(values, SEQ, shifted(group, d))  46.8 us
    pallas_call x2, Pallas kernels, feed(): call(functools.partial(feed_kernel, owned), (steps,), [fixed(rows, width)...  32.7 us
    pallas_call x1, Pallas kernels, attend_back(): call(functools.partial(attend_back_kernel, min(block, (1 << 19) // rows))...  25.3 us
    ppermute x3, waiting for transfers between devices, staged_gather(): lax.ppermute(values, lines.long, shifted(lines.n_long, d))  19.2 us
    ppermute x10, starting transfers between devices, to_next(): return lax.ppermute(values, SEQ, shifted(group, d))  15.6 us
    pallas_call x1, Pallas kernels, attend(): call(functools.partial(attend_kernel, min(block, (1 << 19) // rows)), (pa...  14.8 us
    pallas_call x1, Pallas kernels, project(): call(functools.partial(project_kernel, group), (3,), [fixed(tokens, depth...  13.9 us
    pallas_call x2, Pallas kernels, project_back(): call(project_back_kernel, (2,), [pl.BlockSpec((block, width), lambda i: (...  11 us
  transfers between devices with their start and end apart: 32, of which 15 were waited for; matrix products, arithmetic and copies ran while one was open for 4% of the time, Pallas kernels for 43%

commit v1 on v0

--- a/solution.py
+++ b/solution.py
@@ -162,9 +162,13 @@
             out[...] = total.astype(BF)
 
 
-def add_last_kernel(*refs):
-    *ins, out = refs
-    out[...] = functools.reduce(jnp.add, [r[...].astype(F32) for r in ins]).astype(BF)
+def add_last_kernel(count, *refs):
+    ins, beside, out = refs[:count], refs[count:-1], refs[-1]
+    at = 0
+    for ref in beside:
+        out[:, at : at + ref.shape[1]] = ref[...]
+        at += ref.shape[1]
+    out[:, at:] = functools.reduce(jnp.add, [r[...].astype(F32) for r in ins]).astype(BF)
 
 
 class StagedSum:
@@ -217,16 +221,17 @@
         self.parts += [lax.ppermute(parts[d], lines.long, shifted(lines.n_long, d)) for d in range(1, lines.n_long)]
         return parts
 
-    def last(self):
+    def last(self, beside=()):
+        columns = self.columns + sum(v.shape[1] for v in beside)
         return call(
-            add_last_kernel,
+            functools.partial(add_last_kernel, len(self.parts)),
             (1,),
-            [fixed(self.rows, self.columns)] * len(self.parts),
-            fixed(self.rows, self.columns),
-            shape((self.rows, self.columns), BF),
+            [fixed(self.rows, self.columns)] * len(self.parts) + [fixed(*v.shape) for v in beside],
+            fixed(self.rows, columns),
+            shape((self.rows, columns), BF),
             self.size,
             3 * self.size,
-        )(*self.parts)
+        )(*self.parts, *beside)
 
 
 def share_kernel(group, here, qkv_ref, up_ref, down_ref, out_ref, *refs):
@@ -618,7 +623,7 @@
     column_sums(sums_ref, dn * normal, dn, branch.astype(F32), og)
 
 
-def hidden_back(here, dn, dn_far, hidden, og, gain, weight, at, block=256):
+def hidden_back(here, dn, dn_far, hidden, og, gain, weight, at, block=128):
     rows, width = hidden.shape
     group = 1 + len(dn_far)
     row = pl.BlockSpec((block, width), lambda i, h: (i, 0))
@@ -855,7 +860,7 @@
     deal(here, small_ref[...].T.astype(BF), keep_ref, send_ref, at)
 
 
-def project_grad(here, lines, x, grads, small, block=512):
+def project_grad(here, lines, x, grads, small, block=256):
     rows, depth = x.shape
     width = grads[0].shape[1]
     owned = depth // (2 * lines.chips)
@@ -997,8 +1002,8 @@
     late = take(take(late, here[2], 3), here[1], 2 if lines.outer_long else 1)
     late = jnp.pad(late.transpose(1, 2, 0), ((0, 0), (0, 0), (0, SMALL - 2)))
     out_sum.arrived = after(out_sum.arrived, before)
-    out_sum.long()
-    qkv_sum.long((late,))
+    qkv_sum.arrived = after(qkv_sum.arrived, out_sum.long())
+    ahead = qkv_sum.long((late,))
     tokens_grad = tokens_back(dn_one[0], dn_one_far, tokens[0], hidden_grad, gain_one)
     block_out = hidden + outs[0] + b_down
     for far in out_far:
@@ -1018,7 +1023,7 @@
         down_total = jnp.concatenate(in_order(from_next(down_sum)), axis=0).astype(F32)
     out_last = out_sum.last()
     qkv_sum.parts = after(qkv_sum.parts, (tokens_grad, block_out, up_total, down_total, out_last))
-    att_sums = jnp.concatenate([out_last, qkv_sum.last()], axis=1)
+    att_sums = qkv_sum.last((out_last,))
     out_total, qkv_total, g1, b1, bo, g2, b2, bd, bq, bu = finish_attention(here, from_next(att_sums), width, counts)
     return (
         block_out[None], tokens_grad[None], g1, b1, qkv_total, bq, out_total, bo, g2, b2, up_total, bu,

time: 348 us -> 343 us (0.986)
  waiting for transfers between devices: 91.5 us -> 84.6 us
    ppermute x6, starting transfers between devices: 9.01 us -> 12.6 us  [long(): lax.ppermute(parts[d], lines.long, shifted(lines.n_long, d))]
    unnamed x94 -> x86, local copies, waits for them, and re-layouts: 8.51 us -> 7.68 us
  transfers between devices with their start and end apart: 32 -> 32, of which waited for: 15 -> 14; matrix products, arithmetic and copies ran while one was open for 4% -> 4% of each run, Pallas kernels for 43% -> 44%
where the time goes in v1:
time: 343 us; the launch traced here: 340 us
  Pallas kernels  179 us (52%)
  waiting for transfers between devices  84.6 us (25%)
  starting transfers between devices  40.3 us (12%)
  between operations  14.5 us (4%)
  local copies, waits for them, and re-layouts  13.7 us (4%)
  other arithmetic  7.94 us (2%)
    ppermute x10, waiting for transfers between devices, to_next(): return lax.ppermute(values, SEQ, shifted(group, d))  44.1 us
    pallas_call x2, Pallas kernels, feed(): call(functools.partial(feed_kernel, owned), (steps,), [fixed(rows, width)...  32.7 us
    pallas_call x1, Pallas kernels, attend_back(): call(functools.partial(attend_back_kernel, min(block, (1 << 19) // rows))...  25.4 us
    ppermute x3, waiting for transfers between devices, staged_gather(): lax.ppermute(values, lines.long, shifted(lines.n_long, d))  19.2 us
    ppermute x10, starting transfers between devices, to_next(): return lax.ppermute(values, SEQ, shifted(group, d))  14.9 us
    pallas_call x1, Pallas kernels, attend(): call(functools.partial(attend_kernel, min(block, (1 << 19) // rows)), (pa...  14.8 us
    pallas_call x1, Pallas kernels, project(): call(functools.partial(project_kernel, group), (3,), [fixed(tokens, depth...  14 us
    ppermute x6, starting transfers between devices, long(): lax.ppermute(parts[d], lines.long, shifted(lines.n_long, d))  12.6 us
  transfers between devices with their start and end apart: 32, of which 14 were waited for; matrix products, arithmetic and copies ran while one was open for 4% of the time, Pallas kernels for 44%

profile of v1, /device:TPU:0, one launch (start us, length us, event | category | flops | bytes accessed | tf_op | source)
XLA Modules:
  0.0 340.4 jit_solution(2995533783851511825)
XLA Ops:
  7.9 3.3 shard_map.299
  11.5 3.0 collective-permute-start
  14.5 1.6 collective-permute-start.1
  16.1 2.6 collective-permute-start.2
  18.7 1.3 collective-permute-start.3
  20.0 1.5 collective-permute-start.4
  21.5 3.1 collective-permute-done.1.refs_1_
  24.6 1.5 collective-permute-start.5
  26.1 16.1 %collective-permute-done.2.refs_2_ = bf16[64,1664]{1,0:T(8,128)(2,1)S(1)} collective-permute-done((bf16[64,1664]{1,0:T(8,128)(2,1)S(1)}, bf16[64,1664]{1,0:T(8,128)(2,1)S(1)}, u32[]{:S(2)}, u32[]{:S(2)}) %collective-permute-start.2) | collective-permute-done | bytes 213024 | tf_op jit(solution)/shard_map/ppermute | solution.py:124
  42.2 1.5 collective-permute-start.6
  44.4 3.6 %fusion.2 = (f32[1024,128]{1,0:T(8,128)}, f32[1024,128]{1,0:T(8,128)}, f32[1024,128]{1,0:T(8,128)}) fusion(f32[128]{0:T(128)S(1)} %copy-done.36, f32[1024]{0:T(1024)S(1)} %bitcast.58, f32[1024]{0:T(1024)S(1)} %bitcast.57, f32[1024]{0:T(1024)S(1)} %bitcast.56, pred[128]{0:T(512)(128)(4,1)S(1)} %copy-done.37, pred[128]{0:T(512)(128)(4,1)S(1)} %copy-done.38, ...), kind=kLoop, calls=%fused_computation.7 | loop fusion | flops 786432 | bytes 1586176 | tf_op jit(solution)/shard_map/jit(_where)/select_n | solution.py:423
  48.0 2.5 collective-permute-done.6.refs_6_
  50.5 2.4 collective-permute-done.7.refs_7_
  53.0 3.5 %shard_map.300 = bf16[4,2,64,1664]{3,2,1,0:T(8,128)(2,1)} custom-call(s32[4]{0:T(128)} %pad_add_fusion.here, bf16[64,1664]{1,0:T(8,128)(2,1)} %get-tuple-element.100.refs_0_, bf16[64,1664]{1,0:T(8,128)(2,1)} %copy-done.18, bf16[64,1664]{1,0:T(8,128)(2,1)} %copy-done.19, bf16[64,1664]{1,0:T(8,128)(2,1)} %copy-done.20, bf16[64,1664]{1,0:T(8,128)(2,1)} %copy-done.21, ...), custom_call_target="tpu_custom_call" | custom-call | bytes 851968 | tf_op jit(solution)/shard_map/pallas_call | solution.py:130
  57.5 2.9 collective-permute-done.8.refs_3_.refs_5_
  60.4 1.2 copy-done.3
  61.6 14.0 %shard_map.301 = (bf16[1024,1536]{1,0:T(8,128)(2,1)}, bf16[1024,1536]{1,0:T(8,128)(2,1)}, bf16[1024,1024]{1,0:T(8,128)(2,1)}, f32[16,1024]{1,0:T(8,128)}) custom-call(s32[4]{0:T(128)} %pad_add_fusion.here, bf16[528,1024]{1,0:T(8,128)(2,1)} %copy-done, bf16[528,1024]{1,0:T(8,128)(2,1)} %copy-done.4, bf16[8,64,1664]{2,1,0:T(8,128)(2,1)} %bitcast.33, ...), custom_call_target="tpu_custom_call" | custom-call | flops 805306368 | bytes 2883584 | tf_op jit(solution)/shard_map/pallas_call | solution.py:392
  75.5 14.8 %shard_map.302 = (bf16[1024,512]{1,0:T(8,128)(2,1)}, f32[1024,512]{1,0:T(8,128)}) custom-call(bf16[1024,1536]{1,0:T(8,128)(2,1)} %get-tuple-element.108.q_ref.k_ref.v_ref, bf16[1024,1536]{1,0:T(8,128)(2,1)} %get-tuple-element.108.q_ref.k_ref.v_ref, bf16[1024,1536]{1,0:T(8,128)(2,1)} %get-tuple-element.108.q_ref.k_ref.v_ref), custom_call_target="tpu_custom_call" | custom-call | flops 2147483648 | bytes 1572864 | tf_op jit(solution)/shard_map/pallas_call | solution.py:517
  90.4 1.5 slice.63
  91.8 1.4 collective-permute-start.10
  93.9 12.2 %collective-permute-done.10.refs_1_ = bf16[512,512]{1,0:T(8,128)(2,1)S(1)} collective-permute-done((bf16[512,512]{1,0:T(8,128)(2,1)S(1)}, bf16[512,512]{1,0:T(8,128)(2,1)S(1)}, u32[]{:S(2)}, u32[]{:S(2)}) %collective-permute-start.10) | collective-permute-done | bytes 524320 | tf_op jit(solution)/shard_map/ppermute | solution.py:907
  106.0 6.2 %all-gather.2.cloned.1.call-done.refs_2_.refs_3_.up_ref.down_ref.refs_5_ = bf16[1024,5120]{1,0:T(8,128)(2,1)} async-done(((bf16[64,5120]{1,0:T(8,128)(2,1)}), bf16[1024,5120]{1,0:T(8,128)(2,1)}) %all-gather.2.cloned.1.call-update) | async-done | bytes 10485776 | tf_op jit(solution)/shard_map/all_gather | solution.py:901
  112.3 5.6 %shard_map.303 = (f32[512,1024]{1,0:T(8,128)}, bf16[512,1024]{1,0:T(8,128)(2,1)}) custom-call(s32[4]{0:T(128)} %pad_add_fusion.here, bf16[1024,512]{1,0:T(8,128)(2,1)} %get-tuple-element.110.refs_0_.o_ref, bf16[512,512]{1,0:T(8,128)(2,1)} %copy-done.11, bf16[1024,5120]{1,0:T(8,128)(2,1)} %all-gather.2.cloned.1.call-done.refs_2_.refs_3_.up_ref.down_ref.refs_5_, ...), custom_call_target="tpu_custom_call" | custom-call | flops 268435456 | bytes 1835008 | tf_op jit(solution)/shard_map/pallas_call | solution.py:588
  117.8 1.5 collective-permute-start.11
  120.2 16.7 %shard_map.304 = (bf16[512,2048]{1,0:T(8,128)(2,1)}, bf16[512,2048]{1,0:T(8,128)(2,1)}, f32[512,1024]{1,0:T(8,128)}, f32[512,1024]{1,0:T(8,128)}, f32[1,2048]{1,0:T(1,128)}) custom-call(bf16[512,1024]{1,0:T(8,128)(2,1)} %get-tuple-element.114.x_ref.refs_0_, bf16[512,1024]{1,0:T(8,128)(2,1)} %bitcast.46, ...), custom_call_target="tpu_custom_call" | custom-call | flops 2147483648 | bytes 4194304 | tf_op jit(solution)/shard_map/pallas_call | solution.py:745
  136.9 6.5 %collective-permute-done.11.x_ref.refs_1_ = bf16[512,1024]{1,0:T(8,128)(2,1)S(1)} collective-permute-done((bf16[512,1024]{1,0:T(8,128)(2,1)}, bf16[512,1024]{1,0:T(8,128)(2,1)S(1)}, u32[]{:S(2)}, u32[]{:S(2)}) %collective-permute-start.11) | collective-permute-done | bytes 1048608 | tf_op jit(solution)/shard_map/ppermute | solution.py:907
  144.4 16.0 %shard_map.305 = (bf16[512,2048]{1,0:T(8,128)(2,1)}, bf16[512,2048]{1,0:T(8,128)(2,1)}, bf16[512,1024]{1,0:T(8,128)(2,1)}, bf16[512,1024]{1,0:T(8,128)(2,1)}, f32[1,2048]{1,0:T(1,128)}) custom-call(bf16[512,1024]{1,0:T(8,128)(2,1)} %copy-done.8, bf16[512,1024]{1,0:T(8,128)(2,1)} %copy-done.7, ...), custom_call_target="tpu_custom_call" | custom-call | flops 2147483648 | bytes 4194304 | tf_op jit(solution)/shard_map/pallas_call | solution.py:745
  160.4 1.5 collective-permute-start.13
  161.9 8.5 %shard_map.306.refs_4_ = bf16[1024,4096]{1,0:T(8,128)(2,1)} custom-call(bf16[512,2048]{1,0:T(8,128)(2,1)} %get-tuple-element.122.refs_0_, bf16[512,2048]{1,0:T(8,128)(2,1)} %get-tuple-element.123.refs_1_, bf16[512,1024]{1,0:T(8,128)(2,1)} %bitcast.47, bf16[512,1024]{1,0:T(8,128)(2,1)} %copy-done.7), custom_call_target="tpu_custom_call" | custom-call | flops 1073741824 | bytes 2621440 | tf_op jit(solution)/shard_map/pallas_call | solution.py:789
  170.4 8.7 %shard_map.307 = bf16[1024,4096]{1,0:T(8,128)(2,1)} custom-call(bf16[512,1024]{1,0:T(8,128)(2,1)} %get-tuple-element.114.x_ref.refs_0_, bf16[512,1024]{1,0:T(8,128)(2,1)} %copy-done.8, bf16[512,2048]{1,0:T(8,128)(2,1)} %get-tuple-element.120.refs_2_, bf16[512,2048]{1,0:T(8,128)(2,1)} %get-tuple-element.121.refs_3_, ...), custom_call_target="tpu_custom_call", output_to_operand_aliasing={{}: (4, {})} | custom-call | flops 4294967296 | bytes 10485760 | tf_op jit(solution)/shard_map/pallas_call | solution.py:802
  179.1 6.0 %collective-permute-done.13.refs_1_ = bf16[512,1024]{1,0:T(8,128)(2,1)S(1)} collective-permute-done((bf16[512,1024]{1,0:T(8,128)(2,1)}, bf16[512,1024]{1,0:T(8,128)(2,1)S(1)}, u32[]{:S(2)}, u32[]{:S(2)}) %collective-permute-start.13) | collective-permute-done | bytes 1048608 | tf_op jit(solution)/shard_map/ppermute | solution.py:907
  186.1 10.1 %shard_map.308 = (f32[512,1024]{1,0:T(8,128)}, bf16[512,1024]{1,0:T(8,128)(2,1)}, f32[8,1024]{1,0:T(8,128)}, bf16[512,512]{1,0:T(8,128)(2,1)}, bf16[512,512]{1,0:T(8,128)(2,1)}) custom-call(s32[4]{0:T(128)} %pad_add_fusion.here, f32[512,1024]{1,0:T(8,128)} %get-tuple-element.124.refs_0_, bf16[512,1024]{1,0:T(8,128)(2,1)} %copy-done.41, ...), custom_call_target="tpu_custom_call" | custom-call | flops 214748364800 | bytes 2306867200 | tf_op jit(solution)/shard_map/pallas_call | solution.py:631
  196.2 6.1 %shard_map.309 = (bf16[8,64,1024]{2,1,0:T(8,128)(2,1)}, bf16[8,64,1024]{2,1,0:T(8,128)(2,1)}) custom-call(s32[4]{0:T(128)} %pad_add_fusion.here, bf16[1024,512]{1,0:T(8,128)(2,1)} %get-tuple-element.110.refs_0_.o_ref, bf16[512,512]{1,0:T(8,128)(2,1)} %copy-done.11, bf16[512,1024]{1,0:T(8,128)(2,1)} %get-tuple-element.128.refs_2_), custom_call_target="tpu_custom_call" | custom-call | flops 268435456 | bytes 1048576 | tf_op jit(solution)/shard_map/pallas_call | solution.py:843
  202.3 1.4 collective-permute-start.14
  204.8 12.4 %collective-permute-done.14 = bf16[512,512]{1,0:T(8,128)(2,1)S(1)} collective-permute-done((bf16[512,512]{1,0:T(8,128)(2,1)}, bf16[512,512]{1,0:T(8,128)(2,1)S(1)}, u32[]{:S(2)}, u32[]{:S(2)}) %collective-permute-start.14) | collective-permute-done | bytes 524320 | tf_op jit(solution)/shard_map/ppermute | solution.py:907
  217.3 1.0 pad_maximum_fusion.1.do_ref
  219.3 2.8 shard_map.310
  222.2 25.4 %shard_map.311 = (bf16[1024,512]{1,0:T(8,128)(2,1)}, bf16[1024,512]{1,0:T(8,128)(2,1)}, bf16[1024,512]{1,0:T(8,128)(2,1)}, f32[8,512]{1,0:T(8,128)}) custom-call(bf16[1024,1536]{1,0:T(8,128)(2,1)} %get-tuple-element.108.q_ref.k_ref.v_ref, bf16[1024,1536]{1,0:T(8,128)(2,1)} %get-tuple-element.108.q_ref.k_ref.v_ref, ...), custom_call_target="tpu_custom_call" | custom-call | flops 5368709120 | bytes 2621440 | tf_op jit(solution)/shard_map/pallas_call | solution.py:532
  249.6 8.3 %shard_map.312 = (bf16[8,64,1664]{2,1,0:T(8,128)(2,1)}, bf16[8,64,1664]{2,1,0:T(8,128)(2,1)}) custom-call(s32[4]{0:T(128)} %pad_add_fusion.here, bf16[1024,1024]{1,0:T(8,128)(2,1)} %get-tuple-element.138.x_ref, bf16[1024,512]{1,0:T(8,128)(2,1)} %get-tuple-element.151.dq_ref, bf16[1024,512]{1,0:T(8,128)(2,1)} %get-tuple-element.152.dk_ref, ...), custom_call_target="tpu_custom_call" | custom-call | flops 805306368 | bytes 2162688 | tf_op jit(solution)/shard_map/pallas_call | solution.py:870
  257.9 5.3 %shard_map.313 = (bf16[512,1024]{1,0:T(8,128)(2,1)}, f32[8,1024]{1,0:T(8,128)}) custom-call(bf16[1024,512]{1,0:T(8,128)(2,1)} %get-tuple-element.151.dq_ref, bf16[1024,512]{1,0:T(8,128)(2,1)} %get-tuple-element.152.dk_ref, bf16[1024,512]{1,0:T(8,128)(2,1)} %get-tuple-element.153.dv_ref, bf16[1024,1536]{1,0:T(8,128)(2,1)} %get-tuple-element.147.w_ref, ...), custom_call_target="tpu_custom_call" | custom-call | flops 402653184 | bytes 1966080 | tf_op jit(solution)/shard_map/pallas_call | solution.py:683
  263.3 1.5 collective-permute-start.18
  264.8 1.2 copy-done.2
  266.0 3.2 shard_map.314
  269.1 1.8 collective-permute-start.19
  270.9 5.6 %shard_map.315 = (f32[512,1024]{1,0:T(8,128)}, f32[8,1024]{1,0:T(8,128)}) custom-call(bf16[1024,512]{1,0:T(8,128)(2,1)} %get-tuple-element.151.dq_ref, bf16[1024,512]{1,0:T(8,128)(2,1)} %get-tuple-element.152.dk_ref, bf16[1024,512]{1,0:T(8,128)(2,1)} %get-tuple-element.153.dv_ref, bf16[1024,1536]{1,0:T(8,128)(2,1)} %get-tuple-element.147.w_ref, ...), custom_call_target="tpu_custom_call" | custom-call | flops 402653184 | bytes 1966080 | tf_op jit(solution)/shard_map/pallas_call | solution.py:683
  277.3 1.2 collective-permute-done.20
  278.8 3.0 shard_map.317
  281.8 3.1 collective-permute-start.26
  284.9 2.2 collective-permute-start.27
  287.1 4.5 %collective-permute-done.21 = f32[8,1024]{1,0:T(8,128)S(1)} collective-permute-done((f32[8,1024]{1,0:T(8,128)S(1)}, f32[8,1024]{1,0:T(8,128)S(1)}, u32[]{:S(2)}, u32[]{:S(2)}) %collective-permute-start.21) | collective-permute-done | bytes 32800 | tf_op jit(solution)/shard_map/ppermute | solution.py:999
  291.5 1.5 collective-permute-start.25
  293.9 3.3 collective-permute-start.28
  297.3 3.9 %shard_map.318 = (bf16[64,1664]{1,0:T(8,128)(2,1)}, bf16[64,1664]{1,0:T(8,128)(2,1)}, bf16[64,1664]{1,0:T(8,128)(2,1)}, bf16[64,1664]{1,0:T(8,128)(2,1)}) custom-call(s32[4]{0:T(128)} %pad_add_fusion.here, bf16[4,2,64,1664]{3,2,1,0:T(8,128)(2,1)} %bitcast.39, bf16[4,2,64,1664]{3,2,1,0:T(8,128)(2,1)} %bitcast.41, bf16[4,1,64,1664]{3,2,1,0:T(8,128)(2,1)} %copy-done.13, ...), custom_call_target="tpu_custom_call" | custom-call | flops 319488 | bytes 851968 | tf_op jit(solution)/shard_map/pallas_call | solution.py:208
  301.3 1.4 collective-permute-start.23
  302.7 2.4 collective-permute-start.24
  305.1 1.6 add_convert_fusion
  306.7 4.5 %shard_map.316 = f32[512,1024]{1,0:T(8,128)} custom-call(f32[512,1024]{1,0:T(8,128)} %get-tuple-element.154.refs_0_, bf16[512,1024]{1,0:T(8,128)(2,1)} %copy-done.12, bf16[512,1024]{1,0:T(8,128)(2,1)} %bitcast.36, f32[512,1024]{1,0:T(8,128)} %get-tuple-element.155.refs_3_, f32[1,1024]{1,0:T(1,128)} %get-tuple-element.184.refs_4_), custom_call_target="tpu_custom_call" | custom-call | flops 2621440 | bytes 1835008 | tf_op jit(solution)/shard_map/pallas_call | solution.py:657
  311.9 1.8 shard_map.320.refs_4_
  313.8 3.3 shard_map.319
  317.1 1.5 collective-permute-done.23.refs_2_
  319.4 2.1 shard_map.321.refs_0_
  321.5 1.4 collective-permute-start.29
  322.9 7.0 %collective-permute-done.29.refs_1_ = bf16[64,2688]{1,0:T(8,128)(2,1)S(1)} collective-permute-done((bf16[64,2688]{1,0:T(8,128)(2,1)}, bf16[64,2688]{1,0:T(8,128)(2,1)S(1)}, u32[]{:S(2)}, u32[]{:S(2)}) %collective-permute-start.29) | collective-permute-done | bytes 344096 | tf_op jit(solution)/shard_map/ppermute | solution.py:907
  330.6 2.9 shard_map.322
  (158 shorter events, 14.3 us)
Async XLA Ops:
  7.2 4.1 %copy-start.30 = (s32[3,1,512]{2,1,0:T(1,128)S(1)}, s32[3,1,512]{2,1,0:T(1,128)}, u32[]{:S(2)}) copy-start(s32[3,1,512]{2,1,0:T(1,128)} %param.21) | copy-start | bytes 18436
  7.2 4.2 %copy-start.1 = (bf16[1,512,1024]{2,1,0:T(8,128)(2,1)S(1)}, bf16[1,512,1024]{2,1,0:T(8,128)(2,1)}, u32[]{:S(2)}) copy-start(bf16[1,512,1024]{2,1,0:T(8,128)(2,1)} %param.20) | copy-start | bytes 3145732
  7.2 105.1 %all-gather.2.cloned.1.call-start = ((), (), s32[]{:S(2)}) async-start(), calls=%async_computation.1 | async-start | bytes 11141120 | tf_op jit(solution)/shard_map/all_gather | solution.py:901
  7.9 36.4 %copy-start.36 = (f32[128]{0:T(128)S(1)}, f32[128]{0:T(128)}, u32[]{:S(2)}) copy-start(f32[128]{0:T(128)} %constant.72.clone) | copy-start | bytes 1540
  7.9 36.4 %copy-start.37 = (pred[128]{0:T(512)(128)(4,1)S(1)}, pred[128]{0:T(512)(128)(4,1)}, u32[]{:S(2)}) copy-start(pred[128]{0:T(512)(128)(4,1)} %constant.74.clone) | copy-start | bytes 388
  7.9 36.4 %copy-start.38 = (pred[128]{0:T(512)(128)(4,1)S(1)}, pred[128]{0:T(512)(128)(4,1)}, u32[]{:S(2)}) copy-start(pred[128]{0:T(512)(128)(4,1)} %constant.70.clone) | copy-start | bytes 388
  7.9 36.4 %copy-start.39 = (pred[128]{0:T(512)(128)(4,1)S(1)}, pred[128]{0:T(512)(128)(4,1)}, u32[]{:S(2)}) copy-start(pred[128]{0:T(512)(128)(4,1)} %constant.71.clone) | copy-start | bytes 388
  7.9 36.4 %copy-start.40 = (pred[128]{0:T(512)(128)(4,1)S(1)}, pred[128]{0:T(512)(128)(4,1)}, u32[]{:S(2)}) copy-start(pred[128]{0:T(512)(128)(4,1)} %constant.73.clone) | copy-start | bytes 388
  11.2 3.3 copy-start.17
  11.2 280.3 %reduce-scatter.2.cloned.1.call-start = ((), (), s32[]{:S(2)}) async-start(), calls=%async_computation.2 | async-start | bytes 8912896 | tf_op jit(solution)/shard_map/reduce_scatter | solution.py:904
  11.5 45.0 %copy-start = (bf16[528,1024]{1,0:T(8,128)(2,1)}, bf16[528,1024]{1,0:T(8,128)(2,1)S(1)}, u32[]{:S(2)}) copy-start(bf16[528,1024]{1,0:T(8,128)(2,1)S(1)} %pad_maximum_fusion.refs_0_.tokens_ref) | copy-start | bytes 3244036
  11.5 32.8 %collective-permute-start = (bf16[528,1024]{1,0:T(8,128)(2,1)S(1)}, bf16[528,1024]{1,0:T(8,128)(2,1)S(1)}, u32[]{:S(2)}, u32[]{:S(2)}) collective-permute-start(bf16[528,1024]{1,0:T(8,128)(2,1)S(1)} %pad_maximum_fusion.refs_0_.tokens_ref), channel_id=1, source_target_pairs={{0,1},{1,0},{2,3},{3,2},{4,5},{5,4},{6,7},{7,6},{8,9},{9,8},{10,11... | collective-permute-start | bytes 3244040 | tf_op jit(solution)/shard_map/ppermute | solution.py:907
  14.5 10.1 %collective-permute-start.1 = (bf16[64,1664]{1,0:T(8,128)(2,1)S(1)}, bf16[64,1664]{1,0:T(8,128)(2,1)S(1)}, u32[]{:S(2)}, u32[]{:S(2)}) collective-permute-start(bf16[64,1664]{1,0:T(8,128)(2,1)S(1)} %copy-done.17), channel_id=1, source_target_pairs={{0,8},{8,16},{16,24},{24,0},{1,9},{9,17},{17,25},{25,1},{2,10},{10... | collective-permute-start | bytes 638984 | tf_op jit(solution)/shard_map/ppermute | solution.py:124
  16.1 26.1 %collective-permute-start.2 = (bf16[64,1664]{1,0:T(8,128)(2,1)S(1)}, bf16[64,1664]{1,0:T(8,128)(2,1)S(1)}, u32[]{:S(2)}, u32[]{:S(2)}) collective-permute-start(bf16[64,1664]{1,0:T(8,128)(2,1)S(1)} %copy-done.17), channel_id=1, source_target_pairs={{0,16},{8,24},{16,0},{24,8},{1,17},{9,25},{17,1},{25,9},{2,18},{10... | collective-permute-start | bytes 638984 | tf_op jit(solution)/shard_map/ppermute | solution.py:124
  18.7 25.0 %collective-permute-start.3 = (bf16[64,1664]{1,0:T(8,128)(2,1)S(1)}, bf16[64,1664]{1,0:T(8,128)(2,1)S(1)}, u32[]{:S(2)}, u32[]{:S(2)}) collective-permute-start(bf16[64,1664]{1,0:T(8,128)(2,1)S(1)} %copy-done.17), channel_id=1, source_target_pairs={{0,24},{8,0},{16,8},{24,16},{1,25},{9,1},{17,9},{25,17},{2,26},{10... | collective-permute-start | bytes 638984 | tf_op jit(solution)/shard_map/ppermute | solution.py:124
  20.0 27.9 %collective-permute-start.4 = (bf16[64,1664]{1,0:T(8,128)(2,1)S(1)}, bf16[64,1664]{1,0:T(8,128)(2,1)S(1)}, u32[]{:S(2)}, u32[]{:S(2)}) collective-permute-start(bf16[64,1664]{1,0:T(8,128)(2,1)S(1)} %copy-done.17), channel_id=1, source_target_pairs={{0,4},{4,0},{1,5},{5,1},{2,6},{6,2},{3,7},{7,3},{8,12},{12,8},{9,1... | collective-permute-start | bytes 638984 | tf_op jit(solution)/shard_map/ppermute | solution.py:127
  24.6 28.3 %copy-start.18 = (bf16[64,1664]{1,0:T(8,128)(2,1)}, bf16[64,1664]{1,0:T(8,128)(2,1)S(1)}, u32[]{:S(2)}) copy-start(bf16[64,1664]{1,0:T(8,128)(2,1)S(1)} %collective-permute-done.1.refs_1_) | copy-start | bytes 638980
  24.6 23.4 %collective-permute-start.5 = (bf16[64,1664]{1,0:T(8,128)(2,1)S(1)}, bf16[64,1664]{1,0:T(8,128)(2,1)S(1)}, u32[]{:S(2)}, u32[]{:S(2)}) collective-permute-start(bf16[64,1664]{1,0:T(8,128)(2,1)S(1)} %collective-permute-done.1.refs_1_), channel_id=1, source_target_pairs={{0,4},{4,0},{1,5},{5,1},{2,6},{6,2},{3,7},{7,3},{8,12},{12,8},{9,1... | collective-permute-start | bytes 638984 | tf_op jit(solution)/shard_map/ppermute | solution.py:127
  42.2 10.7 %copy-start.19 = (bf16[64,1664]{1,0:T(8,128)(2,1)}, bf16[64,1664]{1,0:T(8,128)(2,1)S(1)}, u32[]{:S(2)}) copy-start(bf16[64,1664]{1,0:T(8,128)(2,1)S(1)} %collective-permute-done.2.refs_2_) | copy-start | bytes 638980
  42.2 8.3 %collective-permute-start.6 = (bf16[64,1664]{1,0:T(8,128)(2,1)S(1)}, bf16[64,1664]{1,0:T(8,128)(2,1)}, u32[]{:S(2)}, u32[]{:S(2)}) collective-permute-start(bf16[64,1664]{1,0:T(8,128)(2,1)S(1)} %collective-permute-done.2.refs_2_), channel_id=1, source_target_pairs={{0,4},{4,0},{1,5},{5,1},{2,6},{6,2},{3,7},{7,3},{8,12},{12,8},{9,1... | collective-permute-start | bytes 638984 | tf_op jit(solution)/shard_map/ppermute | solution.py:127
  43.7 9.2 %copy-start.20 = (bf16[64,1664]{1,0:T(8,128)(2,1)}, bf16[64,1664]{1,0:T(8,128)(2,1)S(1)}, u32[]{:S(2)}) copy-start(bf16[64,1664]{1,0:T(8,128)(2,1)S(1)} %collective-permute-done.3.refs_3_) | copy-start | bytes 638980
  43.7 9.2 %collective-permute-start.7 = (bf16[64,1664]{1,0:T(8,128)(2,1)S(1)}, bf16[64,1664]{1,0:T(8,128)(2,1)}, u32[]{:S(2)}, u32[]{:S(2)}) collective-permute-start(bf16[64,1664]{1,0:T(8,128)(2,1)S(1)} %collective-permute-done.3.refs_3_), channel_id=1, source_target_pairs={{0,4},{4,0},{1,5},{5,1},{2,6},{6,2},{3,7},{7,3},{8,12},{12,8},{9,1... | collective-permute-start | bytes 638984 | tf_op jit(solution)/shard_map/ppermute | solution.py:127
  44.3 12.3 %copy-start.4 = (bf16[528,1024]{1,0:T(8,128)(2,1)}, bf16[528,1024]{1,0:T(8,128)(2,1)S(1)}, u32[]{:S(2)}) copy-start(bf16[528,1024]{1,0:T(8,128)(2,1)S(1)} %collective-permute-done.refs_1_.tokens_ref) | copy-start | bytes 3244036
  48.0 8.6 %copy-start.6 = (bf16[1,512,1024]{2,1,0:T(8,128)(2,1)S(1)}, bf16[1,512,1024]{2,1,0:T(8,128)(2,1)}, u32[]{:S(2)}) copy-start(bf16[1,512,1024]{2,1,0:T(8,128)(2,1)} %param.34) | copy-start | bytes 3145732
  48.0 5.0 %copy-start.21 = (bf16[64,1664]{1,0:T(8,128)(2,1)}, bf16[64,1664]{1,0:T(8,128)(2,1)S(1)}, u32[]{:S(2)}) copy-start(bf16[64,1664]{1,0:T(8,128)(2,1)S(1)} %collective-permute-done.4.refs_4_) | copy-start | bytes 638980
  48.0 5.0 %copy-start.22 = (bf16[64,1664]{1,0:T(8,128)(2,1)}, bf16[64,1664]{1,0:T(8,128)(2,1)S(1)}, u32[]{:S(2)}) copy-start(bf16[64,1664]{1,0:T(8,128)(2,1)S(1)} %collective-permute-done.5.refs_5_) | copy-start | bytes 638980
  56.5 3.9 %collective-permute-start.8 = (bf16[8,64,1664]{2,1,0:T(8,128)(2,1)}, bf16[8,64,1664]{2,1,0:T(8,128)(2,1)S(1)}, u32[]{:S(2)}, u32[]{:S(2)}) collective-permute-start(bf16[8,64,1664]{2,1,0:T(8,128)(2,1)} %bitcast.32), channel_id=1, source_target_pairs={{0,2},{2,0},{1,3},{3,1},{4,6},{6,4},{5,7},{7,5},{8,10},{10,8},{9,1... | collective-permute-start | bytes 5111816 | tf_op jit(solution)/shard_map/ppermute | solution.py:142
  56.6 33.7 %collective-permute-start.9 = (bf16[512,1024]{1,0:T(8,128)(2,1)S(1)}, bf16[512,1024]{1,0:T(8,128)(2,1)S(1)}, u32[]{:S(2)}, u32[]{:S(2)}) collective-permute-start(bf16[512,1024]{1,0:T(8,128)(2,1)S(1)} %bitcast.49), channel_id=1, source_target_pairs={{0,1},{1,0},{2,3},{3,2},{4,5},{5,4},{6,7},{7,6},{8,9},{9,8},{10,11... | collective-permute-start | bytes 3145736 | tf_op jit(solution)/shard_map/ppermute | solution.py:907
  75.5 17.7 %copy-start.31 = (f32[16,1024]{1,0:T(8,128)S(1)}, f32[16,1024]{1,0:T(8,128)}, u32[]{:S(2)}) copy-start(f32[16,1024]{1,0:T(8,128)} %get-tuple-element.112) | copy-start | bytes 196612
  90.4 27.5 %copy-start.7 = (bf16[512,1024]{1,0:T(8,128)(2,1)}, bf16[512,1024]{1,0:T(8,128)(2,1)S(1)}, u32[]{:S(2)}) copy-start(bf16[512,1024]{1,0:T(8,128)(2,1)S(1)} %collective-permute-done.9.og_ref.refs_3_) | copy-start | bytes 3145732
  91.8 14.2 %collective-permute-start.10 = (bf16[512,512]{1,0:T(8,128)(2,1)S(1)}, bf16[512,512]{1,0:T(8,128)(2,1)S(1)}, u32[]{:S(2)}, u32[]{:S(2)}) collective-permute-start(bf16[512,512]{1,0:T(8,128)(2,1)S(1)} %slice.63), channel_id=1, source_target_pairs={{0,1},{1,0},{2,3},{3,2},{4,5},{5,4},{6,7},{7,6},{8,9},{9,8},{10,11... | collective-permute-start | bytes 1572872 | tf_op jit(solution)/shard_map/ppermute | solution.py:907
  106.0 6.2 %copy-start.11 = (bf16[512,512]{1,0:T(8,128)(2,1)}, bf16[512,512]{1,0:T(8,128)(2,1)S(1)}, u32[]{:S(2)}) copy-start(bf16[512,512]{1,0:T(8,128)(2,1)S(1)} %collective-permute-done.10.refs_1_) | copy-start | bytes 1572868
  117.8 25.6 %collective-permute-start.11 = (bf16[512,1024]{1,0:T(8,128)(2,1)}, bf16[512,1024]{1,0:T(8,128)(2,1)S(1)}, u32[]{:S(2)}, u32[]{:S(2)}) collective-permute-start(bf16[512,1024]{1,0:T(8,128)(2,1)} %get-tuple-element.114.x_ref.refs_0_), channel_id=1, source_target_pairs={{0,1},{1,0},{2,3},{3,2},{4,5},{5,4},{6,7},{7,6},{8,9},{9,8},{10,11... | collective-permute-start | bytes 3145736 | tf_op jit(solution)/shard_map/ppermute | solution.py:907
  160.4 24.8 %collective-permute-start.13 = (bf16[512,1024]{1,0:T(8,128)(2,1)}, bf16[512,1024]{1,0:T(8,128)(2,1)S(1)}, u32[]{:S(2)}, u32[]{:S(2)}) collective-permute-start(bf16[512,1024]{1,0:T(8,128)(2,1)} %get-tuple-element.125), channel_id=1, source_target_pairs={{0,1},{1,0},{2,3},{3,2},{4,5},{5,4},{6,7},{7,6},{8,9},{9,8},{10,11... | collective-permute-start | bytes 3145736 | tf_op jit(solution)/shard_map/ppermute | solution.py:907
  196.2 8.3 %copy-start.33 = (f32[1,2048]{1,0:T(1,128)S(1)}, f32[1,2048]{1,0:T(1,128)}, u32[]{:S(2)}) copy-start(f32[1,2048]{1,0:T(1,128)} %get-tuple-element.141) | copy-start | bytes 24580
  196.2 8.3 %copy-start.34 = (f32[1,2048]{1,0:T(1,128)S(1)}, f32[1,2048]{1,0:T(1,128)}, u32[]{:S(2)}) copy-start(f32[1,2048]{1,0:T(1,128)} %get-tuple-element.142) | copy-start | bytes 24580
  196.2 8.6 %copy-start.35 = (f32[8,1024]{1,0:T(8,128)S(1)}, f32[8,1024]{1,0:T(8,128)}, u32[]{:S(2)}) copy-start(f32[8,1024]{1,0:T(8,128)} %get-tuple-element.139) | copy-start | bytes 98308
  196.2 21.1 %copy-start.15 = (bf16[512,512]{1,0:T(8,128)(2,1)S(1)}, bf16[512,512]{1,0:T(8,128)(2,1)}, u32[]{:S(2)}) copy-start(bf16[512,512]{1,0:T(8,128)(2,1)} %get-tuple-element.126) | copy-start | bytes 1572868
  202.3 16.0 %collective-permute-start.15 = (bf16[8,64,1024]{2,1,0:T(8,128)(2,1)}, bf16[8,64,1024]{2,1,0:T(8,128)(2,1)S(1)}, u32[]{:S(2)}, u32[]{:S(2)}) collective-permute-start(bf16[8,64,1024]{2,1,0:T(8,128)(2,1)} %get-tuple-element.130), channel_id=1, source_target_pairs={{0,2},{2,0},{1,3},{3,1},{4,6},{6,4},{5,7},{7,5},{8,10},{10,8},{9,1... | collective-permute-start | bytes 3145736 | tf_op jit(solution)/shard_map/ppermute | solution.py:177
  202.3 15.0 %collective-permute-start.14 = (bf16[512,512]{1,0:T(8,128)(2,1)}, bf16[512,512]{1,0:T(8,128)(2,1)S(1)}, u32[]{:S(2)}, u32[]{:S(2)}) collective-permute-start(bf16[512,512]{1,0:T(8,128)(2,1)} %get-tuple-element.127), channel_id=1, source_target_pairs={{0,1},{1,0},{2,3},{3,2},{4,5},{5,4},{6,7},{7,6},{8,9},{9,8},{10,11... | collective-permute-start | bytes 1572872 | tf_op jit(solution)/shard_map/ppermute | solution.py:907
  203.9 45.7 %collective-permute-start.12 = (bf16[512,1024]{1,0:T(8,128)(2,1)}, bf16[512,1024]{1,0:T(8,128)(2,1)S(1)}, u32[]{:S(2)}, u32[]{:S(2)}) collective-permute-start(bf16[512,1024]{1,0:T(8,128)(2,1)} %get-tuple-element.118), channel_id=1, source_target_pairs={{0,1},{1,0},{2,3},{3,2},{4,5},{5,4},{6,7},{7,6},{8,9},{9,8},{10,11... | collective-permute-start | bytes 3145736 | tf_op jit(solution)/shard_map/ppermute | solution.py:907
  222.1 27.5 %collective-permute-start.16 = (bf16[4,1,64,1024]{3,2,1,0:T(8,128)(2,1)}, bf16[4,1,64,1024]{3,2,1,0:T(8,128)(2,1)S(1)}, u32[]{:S(2)}, u32[]{:S(2)}) collective-permute-start(bf16[4,1,64,1024]{3,2,1,0:T(8,128)(2,1)} %shard_map.310), channel_id=1, source_target_pairs={{0,4},{4,0},{1,5},{5,1},{2,6},{6,2},{3,7},{7,3},{8,12},{12,8},{9,1... | collective-permute-start | bytes 1572872 | tf_op jit(solution)/shard_map/ppermute | solution.py:202
  249.6 8.3 %copy-start.14 = (bf16[4,1,64,1024]{3,2,1,0:T(8,128)(2,1)}, bf16[4,1,64,1024]{3,2,1,0:T(8,128)(2,1)S(1)}, u32[]{:S(2)}) copy-start(bf16[4,1,64,1024]{3,2,1,0:T(8,128)(2,1)S(1)} %collective-permute-done.16.refs_0_) | copy-start | bytes 1572868
  257.9 6.9 %collective-permute-start.17 = (bf16[8,64,1664]{2,1,0:T(8,128)(2,1)}, bf16[8,64,1664]{2,1,0:T(8,128)(2,1)S(1)}, u32[]{:S(2)}, u32[]{:S(2)}) collective-permute-start(bf16[8,64,1664]{2,1,0:T(8,128)(2,1)} %get-tuple-element.150), channel_id=1, source_target_pairs={{0,2},{2,0},{1,3},{3,1},{4,6},{6,4},{5,7},{7,5},{8,10},{10,8},{9,1... | collective-permute-start | bytes 5111816 | tf_op jit(solution)/shard_map/ppermute | solution.py:177
  263.3 37.9 %collective-permute-start.18 = (bf16[512,1024]{1,0:T(8,128)(2,1)}, bf16[512,1024]{1,0:T(8,128)(2,1)S(1)}, u32[]{:S(2)}, u32[]{:S(2)}) collective-permute-start(bf16[512,1024]{1,0:T(8,128)(2,1)} %get-tuple-element.148), channel_id=1, source_target_pairs={{0,1},{1,0},{2,3},{3,2},{4,5},{5,4},{6,7},{7,6},{8,9},{9,8},{10,11... | collective-permute-start | bytes 3145736 | tf_op jit(solution)/shard_map/ppermute | solution.py:907
  269.1 7.4 %copy-start.29 = (f32[8,1024]{1,0:T(8,128)S(1)}, f32[8,1024]{1,0:T(8,128)}, u32[]{:S(2)}) copy-start(f32[8,1024]{1,0:T(8,128)} %get-tuple-element.163) | copy-start | bytes 98308
  269.1 24.8 %collective-permute-start.19 = (bf16[4,1,64,1664]{3,2,1,0:T(8,128)(2,1)}, bf16[4,1,64,1664]{3,2,1,0:T(8,128)(2,1)S(1)}, u32[]{:S(2)}, u32[]{:S(2)}) collective-permute-start(bf16[4,1,64,1664]{3,2,1,0:T(8,128)(2,1)} %shard_map.314), channel_id=1, source_target_pairs={{0,4},{4,0},{1,5},{5,1},{2,6},{6,2},{3,7},{7,3},{8,12},{12,8},{9,1... | collective-permute-start | bytes 2555912 | tf_op jit(solution)/shard_map/ppermute | solution.py:202
  277.3 1.2 collective-permute-start.20
  278.5 13.0 %collective-permute-start.21 = (f32[8,1024]{1,0:T(8,128)S(1)}, f32[8,1024]{1,0:T(8,128)S(1)}, u32[]{:S(2)}, u32[]{:S(2)}) collective-permute-start(f32[8,1024]{1,0:T(8,128)S(1)} %add.61), channel_id=1, source_target_pairs={{0,4},{4,0},{1,5},{5,1},{2,6},{6,2},{3,7},{7,3},{8,12},{12,8},{9,1... | collective-permute-start | bytes 98312 | tf_op jit(solution)/shard_map/ppermute | solution.py:999
  281.8 19.5 %collective-permute-start.26 = (bf16[64,1024]{1,0:T(8,128)(2,1)}, bf16[64,1024]{1,0:T(8,128)(2,1)S(1)}, u32[]{:S(2)}, u32[]{:S(2)}) collective-permute-start(bf16[64,1024]{1,0:T(8,128)(2,1)} %get-tuple-element.158), channel_id=1, source_target_pairs={{0,8},{8,16},{16,24},{24,0},{1,9},{9,17},{17,25},{25,1},{2,10},{10... | collective-permute-start | bytes 393224 | tf_op jit(solution)/shard_map/ppermute | solution.py:221
  284.9 17.8 %collective-permute-start.27 = (bf16[64,1024]{1,0:T(8,128)(2,1)}, bf16[64,1024]{1,0:T(8,128)(2,1)S(1)}, u32[]{:S(2)}, u32[]{:S(2)}) collective-permute-start(bf16[64,1024]{1,0:T(8,128)(2,1)} %get-tuple-element.159), channel_id=1, source_target_pairs={{0,16},{8,24},{16,0},{24,8},{1,17},{9,25},{17,1},{25,9},{2,18},{10... | collective-permute-start | bytes 393224 | tf_op jit(solution)/shard_map/ppermute | solution.py:221
  291.5 22.2 %collective-permute-start.25 = (bf16[64,4096]{1,0:T(8,128)(2,1)}, bf16[64,4096]{1,0:T(8,128)(2,1)}, u32[]{:S(2)}, u32[]{:S(2)}) collective-permute-start(bf16[64,4096]{1,0:T(8,128)(2,1)} %reduce-scatter.2.cloned.1.call-done.refs_0_), channel_id=1, source_target_pairs={{0,1},{1,0},{2,3},{3,2},{4,5},{5,4},{6,7},{7,6},{8,9},{9,8},{10,11... | collective-permute-start | bytes 1572872 | tf_op jit(solution)/shard_map/ppermute | solution.py:907
  293.9 3.3 copy-start.13
  293.9 17.4 %collective-permute-start.28 = (bf16[64,1024]{1,0:T(8,128)(2,1)}, bf16[64,1024]{1,0:T(8,128)(2,1)S(1)}, u32[]{:S(2)}, u32[]{:S(2)}) collective-permute-start(bf16[64,1024]{1,0:T(8,128)(2,1)} %get-tuple-element.160), channel_id=1, source_target_pairs={{0,24},{8,0},{16,8},{24,16},{1,25},{9,1},{17,9},{25,17},{2,26},{10... | collective-permute-start | bytes 393224 | tf_op jit(solution)/shard_map/ppermute | solution.py:221
  297.2 7.9 %copy-start.9 = (f32[512,1024]{1,0:T(8,128)S(1)}, f32[512,1024]{1,0:T(8,128)}, u32[]{:S(2)}) copy-start(f32[512,1024]{1,0:T(8,128)} %get-tuple-element.113.refs_2_) | copy-start | bytes 6291460
  297.2 7.9 %copy-start.10 = (f32[512,1024]{1,0:T(8,128)S(1)}, f32[512,1024]{1,0:T(8,128)}, u32[]{:S(2)}) copy-start(f32[512,1024]{1,0:T(8,128)} %get-tuple-element.115) | copy-start | bytes 6291460
  297.3 7.9 %copy-start.32 = (f32[1,1024]{1,0:T(1,128)S(1)}, f32[1,1024]{1,0:T(1,128)}, u32[]{:S(2)}) copy-start(f32[1,1024]{1,0:T(1,128)} %get-tuple-element.185) | copy-start | bytes 12292
  301.2 5.6 %copy-start.12 = (bf16[512,1024]{1,0:T(8,128)(2,1)}, bf16[512,1024]{1,0:T(8,128)(2,1)S(1)}, u32[]{:S(2)}) copy-start(bf16[512,1024]{1,0:T(8,128)(2,1)S(1)} %collective-permute-done.18.refs_1_) | copy-start | bytes 3145732
  301.2 15.9 %collective-permute-start.22 = (bf16[64,1664]{1,0:T(8,128)(2,1)}, bf16[64,1664]{1,0:T(8,128)(2,1)S(1)}, u32[]{:S(2)}, u32[]{:S(2)}) collective-permute-start(bf16[64,1664]{1,0:T(8,128)(2,1)} %get-tuple-element.165), channel_id=1, source_target_pairs={{0,8},{8,16},{16,24},{24,0},{1,9},{9,17},{17,25},{25,1},{2,10},{10... | collective-permute-start | bytes 638984 | tf_op jit(solution)/shard_map/ppermute | solution.py:221
  301.3 5.5 %copy-start.26 = (bf16[64,1024]{1,0:T(8,128)(2,1)}, bf16[64,1024]{1,0:T(8,128)(2,1)S(1)}, u32[]{:S(2)}) copy-start(bf16[64,1024]{1,0:T(8,128)(2,1)S(1)} %collective-permute-done.26.refs_1_) | copy-start | bytes 393220
  301.3 17.4 %collective-permute-start.23 = (bf16[64,1664]{1,0:T(8,128)(2,1)}, bf16[64,1664]{1,0:T(8,128)(2,1)S(1)}, u32[]{:S(2)}, u32[]{:S(2)}) collective-permute-start(bf16[64,1664]{1,0:T(8,128)(2,1)} %get-tuple-element.166), channel_id=1, source_target_pairs={{0,16},{8,24},{16,0},{24,8},{1,17},{9,25},{17,1},{25,9},{2,18},{10... | collective-permute-start | bytes 638984 | tf_op jit(solution)/shard_map/ppermute | solution.py:221
  302.7 4.0 %copy-start.27 = (bf16[64,1024]{1,0:T(8,128)(2,1)}, bf16[64,1024]{1,0:T(8,128)(2,1)S(1)}, u32[]{:S(2)}) copy-start(bf16[64,1024]{1,0:T(8,128)(2,1)S(1)} %collective-permute-done.27.refs_2_) | copy-start | bytes 393220
  302.7 16.0 %collective-permute-start.24 = (bf16[64,1664]{1,0:T(8,128)(2,1)}, bf16[64,1664]{1,0:T(8,128)(2,1)S(1)}, u32[]{:S(2)}, u32[]{:S(2)}) collective-permute-start(bf16[64,1664]{1,0:T(8,128)(2,1)} %get-tuple-element.167), channel_id=1, source_target_pairs={{0,24},{8,0},{16,8},{24,16},{1,25},{9,1},{17,9},{25,17},{2,26},{10... | collective-permute-start | bytes 638984 | tf_op jit(solution)/shard_map/ppermute | solution.py:221
  321.5 8.4 %collective-permute-start.29 = (bf16[64,2688]{1,0:T(8,128)(2,1)}, bf16[64,2688]{1,0:T(8,128)(2,1)S(1)}, u32[]{:S(2)}, u32[]{:S(2)}) collective-permute-start(bf16[64,2688]{1,0:T(8,128)(2,1)} %shard_map.321.refs_0_), channel_id=1, source_target_pairs={{0,1},{1,0},{2,3},{3,2},{4,5},{5,4},{6,7},{7,6},{8,9},{9,8},{10,11... | collective-permute-start | bytes 1032200 | tf_op jit(solution)/shard_map/ppermute | solution.py:907
  (10 other events, 9.7 us)
Sparse Core Ops, SparseCore 0:
  11.4 100.8 all-gather.1
  179.2 106.1 reduce-scatter.1
